TPU v7x, 256 devices: a whole 4x4x8 slice. The times are simulated.
256 devices in a mesh: ctx: 32 (over z_lo, y, x), head: 8 (over z_hi, core).
Axes of the slice: x: 4, y: 4, z: 8 (z_hi: 4, z_lo: 2; z = z_hi * 2 + z_lo), core: 2. Of those that a mesh axis runs over, the one named last changes fastest.
Arguments:
- queries: bfloat16 [16384, 4096], P('ctx', 'head'), may hold values from -240 to 240
- key_rows: bfloat16 [16384, 4, 128], P('ctx'), may hold values from -8 to 8
- value_vectors: bfloat16 [16384, 4, 128], P('ctx'), may hold values from -6 to 6
- out_weight: bfloat16 [4096, 2048], P('head'), may hold values from -0.125 to 0.125
- doc_start: int32 [128], P('ctx'), may hold values from 0 to 127, as said below
- block_list: int32 [32, 35], P('ctx'), may hold values from -1 to 127, as said below
Outputs:
- projected: bfloat16 [16384, 2048], P('ctx', 'head')
Inputs may be any that keep to these rules, and one draw needn't show every extreme that they name: `doc_start`: documents begin on block boundaries and are 1 to 32 blocks long, one of them exactly 32; the last block begins a document of its own. `block_list`: row r holds, ascending, every block from the document start of block r * 4 through block (r + 1) * 4 - 1, and -1 in the slots after.
All inputs are finite; a program needn't handle non-finite values.
Results may differ from a plain program's by a relative error of at most 0.018.
Values may be sent and summed in bfloat16 or wider, within the bound.
No kernel may reach another device: no remote copies, remote signals or barrier semaphores. Data moves between devices by JAX's collectives and lax.ppermute only.
A program may use at most 64 MiB of HBM per device.

v0:
```python
import math

import jax
import jax.numpy as jnp
from jax import lax
from jax.sharding import PartitionSpec as P

QUERY_HEADS = 32
KEY_VALUE_HEADS = 4
HEAD_WIDTH = 128
BLK = 128
REACH = 8


NEGATIVE_FILL = -1e30


def shifted(block, axis, distance):
    devices = range(lax.axis_size(axis))
    route = [(i - distance, i) for i in devices if i - distance in devices]
    return lax.ppermute(block, axis, route)


def make_attend(grouped_queries, query_pos, query_docs, listed, score_scale):

    def attend(running, shard_piece, piece_start):
        run_max, run_sum, run_acc = running
        piece_rows = shard_piece.shape[1]
        key_pos = piece_start + jnp.arange(piece_rows, dtype=jnp.int32)
        key_block = jnp.floor_divide(key_pos, BLK)
        in_list = jnp.any(listed[None, :] == key_block[:, None], axis=1)
        allowed = (
            (key_pos[None, :] <= query_pos[:, None])
            & (key_block[None, :] >= query_docs[:, None])
            & in_list[None, :]
        )
        scores = (
            jnp.einsum(
                "tkgd,skd->kgts",
                grouped_queries,
                shard_piece[0],
                preferred_element_type=jnp.float32,
            )
            * score_scale
        )
        scores = jnp.where(allowed, scores, NEGATIVE_FILL)
        new_max = jnp.maximum(run_max, jnp.max(scores, axis=-1))
        weights = jnp.where(allowed, jnp.exp(scores - new_max[..., None]), 0.0)
        factor = jnp.exp(run_max - new_max)
        new_sum = run_sum * factor + jnp.sum(weights, axis=-1)
        new_acc = run_acc * factor[..., None] + jnp.einsum(
            "kgts,skd->kgtd",
            weights.astype(jnp.bfloat16),
            shard_piece[1],
            preferred_element_type=jnp.float32,
        )
        return (new_max, new_sum, new_acc)

    return attend


def on_device(queries, key_rows, value_vectors, out_weight, doc_start, block_list):
    tok_rows = queries.shape[0]
    head_count = queries.shape[1] // HEAD_WIDTH
    heads_per_group = QUERY_HEADS // KEY_VALUE_HEADS
    kv_heads = max(1, head_count // heads_per_group)
    per_group = head_count // kv_heads
    first_head = lax.axis_index("head") * head_count // heads_per_group
    own_keys = lax.dynamic_slice_in_dim(key_rows, first_head, kv_heads, 1)
    own_values = lax.dynamic_slice_in_dim(value_vectors, first_head, kv_heads, 1)
    paired = jnp.stack([own_keys, own_values])
    grouped_queries = queries.reshape(tok_rows, kv_heads, per_group, HEAD_WIDTH)
    ctx_index = lax.axis_index("ctx")
    query_pos = ctx_index * tok_rows + jnp.arange(tok_rows, dtype=jnp.int32)
    query_docs = jnp.repeat(doc_start, BLK)
    listed = block_list[0]
    attend = make_attend(
        grouped_queries, query_pos, query_docs, listed, 1.0 / math.sqrt(HEAD_WIDTH)
    )
    initial = (
        jnp.full((kv_heads, per_group, tok_rows), NEGATIVE_FILL, jnp.float32),
        jnp.zeros((kv_heads, per_group, tok_rows), jnp.float32),
        jnp.zeros((kv_heads, per_group, tok_rows, HEAD_WIDTH), jnp.float32),
    )
    attn_state = attend(initial, paired, ctx_index * tok_rows)

    def advance(step_index, loop_state):
        moving, running = loop_state
        moving = shifted(moving, "ctx", 1)
        piece_start = (ctx_index - step_index) * tok_rows
        running = attend(running, moving, piece_start)
        return (moving, running)

    attn_state = lax.fori_loop(1, REACH + 1, advance, (paired, attn_state))[1]
    run_max, run_sum, run_acc = attn_state
    heads_out = (
        (run_acc / run_sum[..., None])
        .transpose(2, 0, 1, 3)
        .reshape(tok_rows, head_count * HEAD_WIDTH)
        .astype(jnp.bfloat16)
    )
    partial_value = (
        jnp.dot(heads_out, out_weight, preferred_element_type=jnp.float32)
        .astype(jnp.bfloat16)
        .astype(jnp.float32)
    )
    return lax.psum_scatter(
        partial_value.astype(jnp.bfloat16), "head", scatter_dimension=1, tiled=True
    )


def solution(mesh):
    return jax.shard_map(
        on_device,
        mesh=mesh,
        in_specs=(
            P("ctx", "head"),
            P("ctx", None, None),
            P("ctx", None, None),
            P("head", None),
            P("ctx"),
            P("ctx", None),
        ),
        out_specs=P("ctx", "head"),
        check_vma=False,
    )
```

profile of v0, /device:TPU:32, one launch (start us, length us, event | category | flops | bytes accessed | tf_op | source)
XLA Modules:
  0.0 209.6 jit_solution(3085687652453238851)
XLA Ops:
  7.4 1.7 constant_dynamic-slice_fusion
  9.2 1.3 copy.23
  11.5 2.0 fusion.26
  13.5 1.1 fusion.28
  14.6 2.5 %fusion.36 = f32[1,4,512,128]{3,2,1,0:T(8,128)} fusion(f32[512,512,4]{1,0,2:T(8,128)S(1)} %get-tuple-element.326, f32[4,512]{1,0:T(4,128)S(1)} %get-tuple-element.324, pred[512,512]{0,1:T(8,128)(4,1)S(1)} %and_and_fusion.1, f32[4,512]{1,0:T(4,128)S(1)} %get-tuple-element.322, bf16[512,1,128]{2,1,0:T(2,128)(2,1)S(1)} %get-tuple-element.327), kind=kOutput, calls=%fused_computation.46 | convolution fusion | flops 273940480 | bytes 5652480 | tf_op jit(solution)/shard_map/kgts,skd->kgtd/dot_general | solution.py:51
  17.5 141.7 %while.22 = (s32[]{:T(128)}, bf16[2,512,1,128]{3,1,2,0:T(8,128)(2,1)S(1)}, f32[1,4,512]{2,1,0:T(4,128)S(1)}, f32[1,4,512]{2,1,0:T(4,128)S(1)}, f32[1,4,512,128]{...) while((s32[]{:T(128)}, ...), condition=%wide.region_7.8_spmd.clone, body=%wide.region_3.7_spmd.clone.sunk | while | flops 552125440 | bytes 26627472 | solution.py:94
  17.5 3.4 %collective-permute-start = (bf16[2,512,1,128]{3,1,2,0:T(8,128)(2,1)S(1)}, bf16[2,512,1,128]{3,1,2,0:T(8,128)(2,1)S(1)}, u32[]{:S(2)}, u32[]{:S(2)}) collective-permute-start(bf16[2,512,1,128]{3,1,2,0:T(8,128)(2,1)S(1)} %get-tuple-element.417), channel_id=1, source_target_pairs={{0,8},{8,16},{16,24},{24,32},{32,40},{40,48},{48,56},{56,64},{64,7... | collective-permute-start | bytes 786440 | tf_op jit(solution)/shard_map/while/body/eval_jaxpr/ppermute | solution.py:21
  21.4 10.2 %collective-permute-done = bf16[2,512,1,128]{3,1,2,0:T(8,128)(2,1)S(1)} collective-permute-done((bf16[2,512,1,128]{3,1,2,0:T(8,128)(2,1)S(1)}, bf16[2,512,1,128]{3,1,2,0:T(8,128)(2,1)S(1)}, u32[]{:S(2)}, u32[]{:S(2)}) %collective-permute-start) | collective-permute-done | bytes 262176 | tf_op jit(solution)/shard_map/while/body/eval_jaxpr/ppermute | solution.py:21
  32.6 1.0 fusion.64
  33.7 1.9 fusion.65
  35.6 1.0 copy-done.2
  36.6 1.9 collective-permute-start
  39.0 10.8 %collective-permute-done = bf16[2,512,1,128]{3,1,2,0:T(8,128)(2,1)S(1)} collective-permute-done((bf16[2,512,1,128]{3,1,2,0:T(8,128)(2,1)S(1)}, bf16[2,512,1,128]{3,1,2,0:T(8,128)(2,1)S(1)}, u32[]{:S(2)}, u32[]{:S(2)}) %collective-permute-start) | collective-permute-done | bytes 262176 | tf_op jit(solution)/shard_map/while/body/eval_jaxpr/ppermute | solution.py:21
  50.8 1.0 fusion.64
  51.9 1.9 fusion.65
  53.8 1.0 copy-done.2
  54.8 1.9 collective-permute-start
  57.2 10.0 %collective-permute-done = bf16[2,512,1,128]{3,1,2,0:T(8,128)(2,1)S(1)} collective-permute-done((bf16[2,512,1,128]{3,1,2,0:T(8,128)(2,1)S(1)}, bf16[2,512,1,128]{3,1,2,0:T(8,128)(2,1)S(1)}, u32[]{:S(2)}, u32[]{:S(2)}) %collective-permute-start) | collective-permute-done | bytes 262176 | tf_op jit(solution)/shard_map/while/body/eval_jaxpr/ppermute | solution.py:21
  68.2 1.0 fusion.64
  69.3 1.9 fusion.65
  71.2 1.0 copy-done.2
  72.2 1.9 collective-permute-start
  74.6 10.0 %collective-permute-done = bf16[2,512,1,128]{3,1,2,0:T(8,128)(2,1)S(1)} collective-permute-done((bf16[2,512,1,128]{3,1,2,0:T(8,128)(2,1)S(1)}, bf16[2,512,1,128]{3,1,2,0:T(8,128)(2,1)S(1)}, u32[]{:S(2)}, u32[]{:S(2)}) %collective-permute-start) | collective-permute-done | bytes 262176 | tf_op jit(solution)/shard_map/while/body/eval_jaxpr/ppermute | solution.py:21
  85.6 1.0 fusion.64
  86.7 1.9 fusion.65
  88.6 1.0 copy-done.2
  89.6 1.9 collective-permute-start
  92.0 10.0 %collective-permute-done = bf16[2,512,1,128]{3,1,2,0:T(8,128)(2,1)S(1)} collective-permute-done((bf16[2,512,1,128]{3,1,2,0:T(8,128)(2,1)S(1)}, bf16[2,512,1,128]{3,1,2,0:T(8,128)(2,1)S(1)}, u32[]{:S(2)}, u32[]{:S(2)}) %collective-permute-start) | collective-permute-done | bytes 262176 | tf_op jit(solution)/shard_map/while/body/eval_jaxpr/ppermute | solution.py:21
  103.0 1.0 fusion.64
  104.1 1.9 fusion.65
  106.0 1.0 copy-done.2
  107.0 1.9 collective-permute-start
  109.4 10.0 %collective-permute-done = bf16[2,512,1,128]{3,1,2,0:T(8,128)(2,1)S(1)} collective-permute-done((bf16[2,512,1,128]{3,1,2,0:T(8,128)(2,1)S(1)}, bf16[2,512,1,128]{3,1,2,0:T(8,128)(2,1)S(1)}, u32[]{:S(2)}, u32[]{:S(2)}) %collective-permute-start) | collective-permute-done | bytes 262176 | tf_op jit(solution)/shard_map/while/body/eval_jaxpr/ppermute | solution.py:21
  120.4 1.0 fusion.64
  121.5 1.9 fusion.65
  123.4 1.0 copy-done.2
  124.4 1.9 collective-permute-start
  126.8 10.0 %collective-permute-done = bf16[2,512,1,128]{3,1,2,0:T(8,128)(2,1)S(1)} collective-permute-done((bf16[2,512,1,128]{3,1,2,0:T(8,128)(2,1)S(1)}, bf16[2,512,1,128]{3,1,2,0:T(8,128)(2,1)S(1)}, u32[]{:S(2)}, u32[]{:S(2)}) %collective-permute-start) | collective-permute-done | bytes 262176 | tf_op jit(solution)/shard_map/while/body/eval_jaxpr/ppermute | solution.py:21
  137.8 1.0 fusion.64
  138.9 1.9 fusion.65
  140.8 1.0 copy-done.2
  141.8 1.9 collective-permute-start
  144.2 10.0 %collective-permute-done = bf16[2,512,1,128]{3,1,2,0:T(8,128)(2,1)S(1)} collective-permute-done((bf16[2,512,1,128]{3,1,2,0:T(8,128)(2,1)S(1)}, bf16[2,512,1,128]{3,1,2,0:T(8,128)(2,1)S(1)}, u32[]{:S(2)}, u32[]{:S(2)}) %collective-permute-start) | collective-permute-done | bytes 262176 | tf_op jit(solution)/shard_map/while/body/eval_jaxpr/ppermute | solution.py:21
  155.2 1.0 fusion.64
  156.3 1.9 fusion.65
  159.2 1.6 copy.25
  160.9 2.6 %convolution_convert_fusion = bf16[512,2048]{1,0:T(8,128)(2,1)} fusion(bf16[512,512]{0,1:T(8,128)(2,1)S(1)} %bitcast.155, bf16[512,2048]{1,0:T(8,128)(2,1)S(1)} %copy-done), kind=kOutput, calls=%fused_computation.39 | convolution fusion | flops 1074790400 | bytes 4718592 | tf_op jit(solution)/shard_map/dot_general | solution.py:103
  163.6 39.2 %reduce-scatter.2.cloned.1.call-done = bf16[512,256]{1,0:T(8,128)(2,1)} async-done(((bf16[512,2048]{1,0:T(8,128)(2,1)}), bf16[512,256]{1,0:T(8,128)(2,1)}) %reduce-scatter.2.cloned.1.call-update) | async-done | bytes 262160 | tf_op jit(solution)/shard_map/reduce_scatter | solution.py:107
  (124 shorter events, 14.9 us)
Async XLA Ops:
  6.5 154.4 %copy-start = (bf16[512,2048]{1,0:T(8,128)(2,1)S(1)}, bf16[512,2048]{1,0:T(8,128)(2,1)}, u32[]{:S(2)}) copy-start(bf16[512,2048]{1,0:T(8,128)(2,1)} %param.11) | copy-start | bytes 6291460
  6.5 196.3 %reduce-scatter.2.cloned.1.call-start = ((), (), s32[]{:S(2)}) async-start(), calls=%async_computation.1 | async-start | bytes 2359296 | tf_op jit(solution)/shard_map/reduce_scatter | solution.py:107
  14.6 2.9 %copy-start.3 = (s32[4]{0:T(128)S(1)}, s32[4]{0:T(128)}, u32[]{:S(2)}) copy-start(s32[4]{0:T(128)} %param.12) | copy-start | bytes 52
  14.6 2.9 %copy-start.4 = (s32[1,35]{1,0:T(1,128)S(1)}, s32[1,35]{1,0:T(1,128)}, u32[]{:S(2)}) copy-start(s32[1,35]{1,0:T(1,128)} %param.13) | copy-start | bytes 424
  17.5 14.2 %collective-permute-start = (bf16[2,512,1,128]{3,1,2,0:T(8,128)(2,1)S(1)}, bf16[2,512,1,128]{3,1,2,0:T(8,128)(2,1)S(1)}, u32[]{:S(2)}, u32[]{:S(2)}) collective-permute-start(bf16[2,512,1,128]{3,1,2,0:T(8,128)(2,1)S(1)} %get-tuple-element.417), channel_id=1, source_target_pairs={{0,8},{8,16},{16,24},{24,32},{32,40},{40,48},{48,56},{56,64},{64,7... | collective-permute-start | bytes 786440 | tf_op jit(solution)/shard_map/while/body/eval_jaxpr/ppermute | solution.py:21
  31.7 2.0 copy-start.1
  35.6 1.0 copy-start.2
  36.6 13.3 %collective-permute-start = (bf16[2,512,1,128]{3,1,2,0:T(8,128)(2,1)S(1)}, bf16[2,512,1,128]{3,1,2,0:T(8,128)(2,1)S(1)}, u32[]{:S(2)}, u32[]{:S(2)}) collective-permute-start(bf16[2,512,1,128]{3,1,2,0:T(8,128)(2,1)S(1)} %get-tuple-element.417), channel_id=1, source_target_pairs={{0,8},{8,16},{16,24},{24,32},{32,40},{40,48},{48,56},{56,64},{64,7... | collective-permute-start | bytes 786440 | tf_op jit(solution)/shard_map/while/body/eval_jaxpr/ppermute | solution.py:21
  49.9 2.0 copy-start.1
  53.8 1.0 copy-start.2
  54.8 12.5 %collective-permute-start = (bf16[2,512,1,128]{3,1,2,0:T(8,128)(2,1)S(1)}, bf16[2,512,1,128]{3,1,2,0:T(8,128)(2,1)S(1)}, u32[]{:S(2)}, u32[]{:S(2)}) collective-permute-start(bf16[2,512,1,128]{3,1,2,0:T(8,128)(2,1)S(1)} %get-tuple-element.417), channel_id=1, source_target_pairs={{0,8},{8,16},{16,24},{24,32},{32,40},{40,48},{48,56},{56,64},{64,7... | collective-permute-start | bytes 786440 | tf_op jit(solution)/shard_map/while/body/eval_jaxpr/ppermute | solution.py:21
  67.3 2.0 copy-start.1
  71.2 1.0 copy-start.2
  72.2 12.5 %collective-permute-start = (bf16[2,512,1,128]{3,1,2,0:T(8,128)(2,1)S(1)}, bf16[2,512,1,128]{3,1,2,0:T(8,128)(2,1)S(1)}, u32[]{:S(2)}, u32[]{:S(2)}) collective-permute-start(bf16[2,512,1,128]{3,1,2,0:T(8,128)(2,1)S(1)} %get-tuple-element.417), channel_id=1, source_target_pairs={{0,8},{8,16},{16,24},{24,32},{32,40},{40,48},{48,56},{56,64},{64,7... | collective-permute-start | bytes 786440 | tf_op jit(solution)/shard_map/while/body/eval_jaxpr/ppermute | solution.py:21
  84.7 2.0 copy-start.1
  88.6 1.0 copy-start.2
  89.6 12.5 %collective-permute-start = (bf16[2,512,1,128]{3,1,2,0:T(8,128)(2,1)S(1)}, bf16[2,512,1,128]{3,1,2,0:T(8,128)(2,1)S(1)}, u32[]{:S(2)}, u32[]{:S(2)}) collective-permute-start(bf16[2,512,1,128]{3,1,2,0:T(8,128)(2,1)S(1)} %get-tuple-element.417), channel_id=1, source_target_pairs={{0,8},{8,16},{16,24},{24,32},{32,40},{40,48},{48,56},{56,64},{64,7... | collective-permute-start | bytes 786440 | tf_op jit(solution)/shard_map/while/body/eval_jaxpr/ppermute | solution.py:21
  102.1 2.0 copy-start.1
  106.0 1.0 copy-start.2
  107.0 12.5 %collective-permute-start = (bf16[2,512,1,128]{3,1,2,0:T(8,128)(2,1)S(1)}, bf16[2,512,1,128]{3,1,2,0:T(8,128)(2,1)S(1)}, u32[]{:S(2)}, u32[]{:S(2)}) collective-permute-start(bf16[2,512,1,128]{3,1,2,0:T(8,128)(2,1)S(1)} %get-tuple-element.417), channel_id=1, source_target_pairs={{0,8},{8,16},{16,24},{24,32},{32,40},{40,48},{48,56},{56,64},{64,7... | collective-permute-start | bytes 786440 | tf_op jit(solution)/shard_map/while/body/eval_jaxpr/ppermute | solution.py:21
  119.5 2.0 copy-start.1
  123.4 1.0 copy-start.2
  124.4 12.5 %collective-permute-start = (bf16[2,512,1,128]{3,1,2,0:T(8,128)(2,1)S(1)}, bf16[2,512,1,128]{3,1,2,0:T(8,128)(2,1)S(1)}, u32[]{:S(2)}, u32[]{:S(2)}) collective-permute-start(bf16[2,512,1,128]{3,1,2,0:T(8,128)(2,1)S(1)} %get-tuple-element.417), channel_id=1, source_target_pairs={{0,8},{8,16},{16,24},{24,32},{32,40},{40,48},{48,56},{56,64},{64,7... | collective-permute-start | bytes 786440 | tf_op jit(solution)/shard_map/while/body/eval_jaxpr/ppermute | solution.py:21
  136.9 2.0 copy-start.1
  140.8 1.0 copy-start.2
  141.8 12.5 %collective-permute-start = (bf16[2,512,1,128]{3,1,2,0:T(8,128)(2,1)S(1)}, bf16[2,512,1,128]{3,1,2,0:T(8,128)(2,1)S(1)}, u32[]{:S(2)}, u32[]{:S(2)}) collective-permute-start(bf16[2,512,1,128]{3,1,2,0:T(8,128)(2,1)S(1)} %get-tuple-element.417), channel_id=1, source_target_pairs={{0,8},{8,16},{16,24},{24,32},{32,40},{40,48},{48,56},{56,64},{64,7... | collective-permute-start | bytes 786440 | tf_op jit(solution)/shard_map/while/body/eval_jaxpr/ppermute | solution.py:21
  154.3 2.0 copy-start.1
  158.2 1.0 copy-start.2
Sparse Core Ops, SparseCore 0:
  163.7 39.0 reduce-scatter.1
where the time goes:
time: 212 us; the launch traced here: 210 us
  waiting for transfers between devices  121 us (57%)
  matrix products  29.4 us (14%)
  starting transfers between devices  16.8 us (8%)
  local copies, waits for them, and re-layouts  14.4 us (7%)
  other arithmetic  14.3 us (7%)
  between operations  13.5 us (6%)
    ppermute x8, waiting for transfers between devices, shifted(): return lax.ppermute(block, axis, route)  81.3 us
    reduce_scatter x1, waiting for transfers between devices, on_device(): lax.psum_scatter(partial_value.astype(jnp.bfloat16), 'head', scatter_dime...  39.2 us
    dot_general x9, matrix products, attend(): jnp.einsum('kgts,skd->kgtd', weights.astype(jnp.bfloat16), shard_piece[1]...  17.8 us
    ppermute x8, starting transfers between devices, shifted(): return lax.ppermute(block, axis, route)  16.8 us
    reduce_sum x9, other arithmetic, attend(): new_sum = run_sum * factor + jnp.sum(weights, axis=-1)  9.38 us
    dot_general x9, matrix products, attend(): jnp.einsum('tkgd,skd->kgts', grouped_queries, shard_piece[0], preferred_e...  9.01 us
    while x48, local copies, waits for them, and re-layouts  8.06 us
  transfers between devices with their start and end apart: 9, of which 9 were waited for; matrix products, arithmetic and copies ran while one was open for 2% of the time, Pallas kernels for 0%

commit v1 on v0

v1 whole, which is shorter than its diff:
```python
import functools
import math

import jax
import jax.numpy as jnp
from jax import lax
from jax.experimental import pallas as pl
from jax.experimental.pallas import tpu as pltpu
from jax.sharding import PartitionSpec as P

HEAD_WIDTH = 128
BLK = 128
DOC_BLOCKS = 32
REACH = 8
SHARD = 512
WINDOW = DOC_BLOCKS * BLK
SPAN = (REACH + 1) * SHARD
KEY_TILE = 2048
NEG = -1e30
EXP_SCALE = math.log2(math.e) / math.sqrt(HEAD_WIDTH)
AXES = ("ctx", "head")
SHIFTS = ((1, 5), (2, 6), (3, 7), (4, 8))


def ctx_head_pairs(n_ctx, n_head, route):
    pairs = []
    for c in range(n_ctx):
        for h in range(n_head):
            target = route(c, h)
            if target is not None:
                pairs.append((c * n_head + h, target[0] * n_head + target[1]))
    return pairs


def fetch(block, n_ctx, n_head, by_core):
    def route(c, h):
        d = c + by_core[h % 2]
        return (d, h) if d < n_ctx else None

    return lax.ppermute(block, AXES, ctx_head_pairs(n_ctx, n_head, route))


def swap_cores(block, n_ctx, n_head):
    return lax.ppermute(
        block, AXES, ctx_head_pairs(n_ctx, n_head, lambda c, h: (c, h ^ 1))
    )


def send_piece(block, n_ctx, n_head, dz, dc):
    def route(c, h):
        return (c, (((h // 2 + dz) % (n_head // 2)) * 2) + ((h % 2) ^ dc))

    return lax.ppermute(block, AXES, ctx_head_pairs(n_ctx, n_head, route))


def dot_t(a, b):
    return lax.dot_general(
        a, b, (((1,), (1,)), ((), ())), preferred_element_type=jnp.float32
    )


def attend_kernel(doc_ref, list_ref, q_ref, rq_ref, own_ref, *rest):
    n_sh = len(SHIFTS)
    mine, theirs = rest[:n_sh], rest[n_sh : 2 * n_sh]
    w_ref, rw_ref = rest[2 * n_sh : 2 * n_sh + 2]
    outs = rest[2 * n_sh + 2 : 2 * n_sh + 10]
    kx, vx, qs, ws, ho, bias, sem = rest[2 * n_sh + 10 :]
    ctx = lax.axis_index("ctx")
    head = lax.axis_index("head")
    core = lax.rem(head, 2)
    z = lax.div(head, 2)

    copies = []

    def start(src, dst):
        c = pltpu.make_async_copy(src, dst, sem.at[len(copies)])
        c.start()
        copies.append(c)

    def load_shard(ref, distance):
        row = pl.multiple_of((REACH - distance) * SHARD, SHARD)
        start(ref.at[:SHARD], kx.at[pl.ds(row, SHARD)])
        start(ref.at[SHARD:], vx.at[pl.ds(row, SHARD), pl.ds(0, HEAD_WIDTH)])

    half = pl.multiple_of(core * 256, 256)
    start(q_ref.at[pl.ds(half, 256)], qs.at[:, pl.ds(0, 512)])
    start(rq_ref.at[pl.ds(half, 256)], qs.at[:, pl.ds(512, 512)])
    load_shard(own_ref, 0)
    for (d0, d1), a, b in zip(SHIFTS, mine, theirs):
        load_shard(a, jnp.where(core == 0, d0, d1))
        load_shard(b, jnp.where(core == 0, d1, d0))
    start(w_ref, ws.at[pl.ds(0, 512)])
    start(rw_ref, ws.at[pl.ds(512, 512)])
    vx[:, HEAD_WIDTH:] = jnp.ones((SPAN, HEAD_WIDTH), jnp.bfloat16)

    list_first = list_ref[0, 0]
    list_last = lax.fori_loop(
        0, list_ref.shape[1], lambda i, m: jnp.maximum(m, list_ref[0, i]), -1
    )
    base = (ctx - REACH) * (SHARD // BLK)
    for c in copies[:-2]:
        c.wait()

    def block(ii, carry):
        local = core * 2 + ii
        first = local + 1
        win = pl.multiple_of(first * BLK, BLK)
        row = pl.multiple_of(ii * BLK, BLK)
        lo = jnp.maximum(doc_ref[local], list_first) - base - first
        hi = jnp.minimum(DOC_BLOCKS - 1, list_last - base - first)
        col_block = lax.broadcasted_iota(jnp.int32, (8, WINDOW), 1) // BLK
        bias[...] = jnp.where((col_block >= lo) & (col_block <= hi), 0.0, NEG)
        causal = lax.broadcasted_iota(jnp.int32, (BLK, BLK), 1) <= (
            lax.broadcasted_iota(jnp.int32, (BLK, BLK), 0)
        )
        for g in range(8):
            q = qs[pl.ds(row, BLK), g * HEAD_WIDTH : (g + 1) * HEAD_WIDTH]
            m = None
            for t in range(0, WINDOW, KEY_TILE):
                s = dot_t(q, kx[pl.ds(win + t, KEY_TILE), :])
                s = s + bias[0:1, t : t + KEY_TILE]
                if t + KEY_TILE == WINDOW:
                    s = jnp.concatenate(
                        [s[:, :-BLK], jnp.where(causal, s[:, -BLK:], NEG)], axis=1
                    )
                top = jnp.max(s, axis=1, keepdims=True)
                m_new = top if m is None else jnp.maximum(m, top)
                p = jnp.exp2((s - m_new) * EXP_SCALE).astype(jnp.bfloat16)
                pv = jnp.dot(
                    p,
                    vx[pl.ds(win + t, KEY_TILE), :],
                    preferred_element_type=jnp.float32,
                )
                if m is None:
                    acc = pv
                else:
                    acc = acc * jnp.exp2((m - m_new) * EXP_SCALE) + pv
                m = m_new
            o = acc[:, :HEAD_WIDTH] / acc[:, HEAD_WIDTH:]
            ho[pl.ds(row, BLK), g * HEAD_WIDTH : (g + 1) * HEAD_WIDTH] = o.astype(
                jnp.bfloat16
            )
        return carry

    lax.fori_loop(0, 2, block, 0)
    for c in copies[-2:]:
        c.wait()
    for p in range(8):
        dz, dc = p // 2, p % 2
        target = lax.rem(z + dz, 4) * 2 + lax.rem(core + dc, 2)
        col = pl.multiple_of(target * 256, 256)
        outs[p][...] = jnp.dot(
            ho[...], ws[:, pl.ds(col, 256)], preferred_element_type=jnp.float32
        ).astype(jnp.bfloat16)


def attend(doc_start, block_list, q, rq, own, mine, theirs, w, rw):
    smem = pl.BlockSpec(memory_space=pltpu.SMEM)
    anyspec = pl.BlockSpec(memory_space=pl.ANY)
    vmem = pl.BlockSpec(memory_space=pltpu.VMEM)
    n_arrays = 3 + len(mine) + len(theirs) + 2
    return pl.pallas_call(
        attend_kernel,
        out_shape=[jax.ShapeDtypeStruct((256, 256), jnp.bfloat16)] * 8,
        in_specs=[smem, smem] + [anyspec] * n_arrays,
        out_specs=[vmem] * 8,
        scratch_shapes=[
            pltpu.VMEM((SPAN, HEAD_WIDTH), jnp.bfloat16),
            pltpu.VMEM((SPAN, 2 * HEAD_WIDTH), jnp.bfloat16),
            pltpu.VMEM((256, 1024), jnp.bfloat16),
            pltpu.VMEM((1024, 2048), jnp.bfloat16),
            pltpu.VMEM((256, 1024), jnp.bfloat16),
            pltpu.VMEM((8, WINDOW), jnp.float32),
            pltpu.SemaphoreType.DMA((22,)),
        ],
        compiler_params=pltpu.CompilerParams(vmem_limit_bytes=40 * 2**20),
        cost_estimate=pl.CostEstimate(
            flops=6 * 10**9, bytes_accessed=8 * 2**20, transcendentals=9 * 10**6
        ),
        name="attend",
    )(doc_start, block_list, q, rq, own, *mine, *theirs, w, rw)


def on_device(n_ctx, n_head, queries, key_rows, value_vectors, out_weight, doc_start, block_list):
    head = lax.axis_index("head")
    core = head % 2
    z = head // 2
    swap = functools.partial(swap_cores, n_ctx=n_ctx, n_head=n_head)
    own_k = lax.dynamic_index_in_dim(key_rows, z, 1, keepdims=False)
    own_v = lax.dynamic_index_in_dim(value_vectors, z, 1, keepdims=False)
    own = jnp.concatenate([own_k, own_v], axis=0)
    mine = [fetch(own, n_ctx, n_head, s) for s in SHIFTS]
    rq = swap(queries)
    rw = swap(out_weight)
    theirs = [swap(a) for a in mine]
    pieces = attend(
        doc_start, block_list, queries, rq, own, mine, theirs, out_weight, rw
    )
    got = []
    for p in range(8):
        dz, dc = p // 2, p % 2
        got.append(
            pieces[p]
            if p == 0
            else send_piece(pieces[p], n_ctx, n_head, dz, dc)
        )
    same = sum(g.astype(jnp.float32) for g in got[0::2]).astype(jnp.bfloat16)
    other = sum(g.astype(jnp.float32) for g in got[1::2]).astype(jnp.bfloat16)
    return jnp.where(
        core == 0,
        jnp.concatenate([same, other], axis=0),
        jnp.concatenate([other, same], axis=0),
    )


def solution(mesh):
    n_ctx, n_head = mesh.shape["ctx"], mesh.shape["head"]
    return jax.shard_map(
        functools.partial(on_device, n_ctx, n_head),
        mesh=mesh,
        in_specs=(
            P("ctx", "head"),
            P("ctx", None, None),
            P("ctx", None, None),
            P("head", None),
            P("ctx"),
            P("ctx", None),
        ),
        out_specs=P("ctx", "head"),
        check_vma=False,
    )
```

time: 212 us -> 90.4 us (0.43)
  waiting for transfers between devices: 121 us -> 24.1 us
  matrix products: 29.4 us -> 0 us
  starting transfers between devices: 16.8 us -> 44.2 us
  Pallas kernels: 0 us -> 17.6 us
  between operations: 13.5 us -> 0.16 us
  other arithmetic: 14.3 us -> 0.97 us
  local copies, waits for them, and re-layouts: 14.4 us -> 2.96 us
    ppermute x8 -> x17, waiting for transfers between devices: 81.3 us -> 24.1 us  [the longest x7 18.2 us: send_piece(): return lax.ppermute(block, AXES, ctx_head_pairs(n_ctx, n_head, route))]
    reduce_scatter x1 -> x0, waiting for transfers between devices: 39.2 us -> none  [on_device(): lax.psum_scatter(partial_value.astype(jnp.bfloat16), 'head', scatter_dime...]
    dot_general x19 -> x0, matrix products: 29.4 us -> none  [the longest x9 17.8 us: attend(): jnp.einsum('kgts,skd->kgtd', weights.astype(jnp.bfloat16), shard_piece[1]...]
    ppermute x8 -> x17, starting transfers between devices: 16.8 us -> 44.2 us  [the longest x7 15.9 us: send_piece(): return lax.ppermute(block, AXES, ctx_head_pairs(n_ctx, n_head, route))]
    pallas_call x0 -> x1, Pallas kernels: none -> 17.6 us  [attend(): pl.pallas_call(attend_kernel, out_shape=[jax.ShapeDtypeStruct((256, 256),...]
    while x49 -> x0, local copies, waits for them, and re-layouts: 9.62 us -> none
    reduce_sum x9 -> x0, other arithmetic: 9.38 us -> none  [attend(): new_sum = run_sum * factor + jnp.sum(weights, axis=-1)]
    and x9 -> x0, other arithmetic: 2.8 us -> none  [attend(): (key_pos[None, :] <= query_pos[:, None]) & (key_block[None, :] >= query_d...]
  transfers between devices with their start and end apart: 9 -> 17, of which waited for: 9 -> 8; matrix products, arithmetic and copies ran while one was open for 2% -> 2% of each run, Pallas kernels for 0% -> 0%
where the time goes in v1:
time: 90.4 us; the launch traced here: 90 us
  starting transfers between devices  44.2 us (49%)
  waiting for transfers between devices  24.1 us (27%)
  Pallas kernels  17.6 us (19%)
  local copies, waits for them, and re-layouts  2.96 us (3%)
  other arithmetic  0.97 us (1%)
    ppermute x7, waiting for transfers between devices, send_piece(): return lax.ppermute(block, AXES, ctx_head_pairs(n_ctx, n_head, route))  18.2 us
    pallas_call x1, Pallas kernels, attend(): pl.pallas_call(attend_kernel, out_shape=[jax.ShapeDtypeStruct((256, 256),...  17.6 us
    ppermute x7, starting transfers between devices, send_piece(): return lax.ppermute(block, AXES, ctx_head_pairs(n_ctx, n_head, route))  15.9 us
    ppermute x4, starting transfers between devices, fetch(): return lax.ppermute(block, AXES, ctx_head_pairs(n_ctx, n_head, route))  14.7 us
    ppermute x6, starting transfers between devices, swap_cores(): lax.ppermute(block, AXES, ctx_head_pairs(n_ctx, n_head, lambda c, h: (c,...  13.7 us
    ppermute x4, waiting for transfers between devices, fetch(): return lax.ppermute(block, AXES, ctx_head_pairs(n_ctx, n_head, route))  4.51 us
    dynamic_slice x1, local copies, waits for them, and re-layouts, on_device(): own_v = lax.dynamic_index_in_dim(value_vectors, z, 1, keepdims=False)  1.87 us
  transfers between devices with their start and end apart: 17, of which 8 were waited for; matrix products, arithmetic and copies ran while one was open for 2% of the time, Pallas kernels for 0%

profile of v1, /device:TPU:32, one launch (start us, length us, event | category | flops | bytes accessed | tf_op | source)
XLA Modules:
  0.0 90.0 jit_solution(1740917732689907935)
XLA Ops:
  0.0 0.0 copy-start
  0.0 0.0 copy-start.3
  0.0 0.0 copy-start.2
  0.0 0.1 collective-permute-start.9
  0.1 1.9 %constant_dynamic-slice_fusion = (bf16[512,1,128]{2,1,0:T(2,128)(2,1)S(1)}, bf16[512,1,128]{2,1,0:T(2,128)(2,1)S(1)}) fusion(bf16[512,4,128]{2,1,0:T(4,128)(2,1)} %param.8, s32[]{:T(128)S(6)} %select_n.27, bf16[512,4,128]{2,1,0:T(4,128)(2,1)} %param.7), kind=kLoop, calls=%fused_computation.6 | loop fusion | bytes 524292 | tf_op jit(solution)/shard_map/jit(dynamic_index_in_dim)/dynamic_slice | solution.py:190
  2.1 3.5 %collective-permute-start.4 = (bf16[1024,128]{1,0:T(8,128)(2,1)S(1)}, bf16[1024,128]{1,0:T(8,128)(2,1)S(1)}, u32[]{:S(2)}, u32[]{:S(2)}) collective-permute-start(bf16[1024,128]{1,0:T(8,128)(2,1)S(1)} %pad_maximum_fusion.own_ref), channel_id=1, source_target_pairs={{0,32},{1,65},{2,34},{3,67},{4,36},{5,69},{6,38},{7,71},{8,40},{9,... | collective-permute-start | bytes 786440 | tf_op jit(solution)/shard_map/ppermute | solution.py:40
  5.6 4.7 %collective-permute-start.3 = (bf16[1024,128]{1,0:T(8,128)(2,1)S(1)}, bf16[1024,128]{1,0:T(8,128)(2,1)S(1)}, u32[]{:S(2)}, u32[]{:S(2)}) collective-permute-start(bf16[1024,128]{1,0:T(8,128)(2,1)S(1)} %pad_maximum_fusion.own_ref), channel_id=1, source_target_pairs={{0,24},{1,57},{2,26},{3,59},{4,28},{5,61},{6,30},{7,63},{8,32},{9,... | collective-permute-start | bytes 786440 | tf_op jit(solution)/shard_map/ppermute | solution.py:40
  10.3 3.7 %collective-permute-start.2 = (bf16[1024,128]{1,0:T(8,128)(2,1)S(1)}, bf16[1024,128]{1,0:T(8,128)(2,1)S(1)}, u32[]{:S(2)}, u32[]{:S(2)}) collective-permute-start(bf16[1024,128]{1,0:T(8,128)(2,1)S(1)} %pad_maximum_fusion.own_ref), channel_id=1, source_target_pairs={{0,16},{1,49},{2,18},{3,51},{4,20},{5,53},{6,22},{7,55},{8,24},{9,... | collective-permute-start | bytes 786440 | tf_op jit(solution)/shard_map/ppermute | solution.py:40
  14.0 2.8 %collective-permute-start.1 = (bf16[1024,128]{1,0:T(8,128)(2,1)S(1)}, bf16[1024,128]{1,0:T(8,128)(2,1)S(1)}, u32[]{:S(2)}, u32[]{:S(2)}) collective-permute-start(bf16[1024,128]{1,0:T(8,128)(2,1)S(1)} %pad_maximum_fusion.own_ref), channel_id=1, source_target_pairs={{0,8},{1,41},{2,10},{3,43},{4,12},{5,45},{6,14},{7,47},{8,16},{9,4... | collective-permute-start | bytes 786440 | tf_op jit(solution)/shard_map/ppermute | solution.py:40
  16.8 0.0 collective-permute-done.4.rest_3_
  16.8 12.8 %collective-permute-start.8 = (bf16[1024,128]{1,0:T(8,128)(2,1)S(1)}, bf16[1024,128]{1,0:T(8,128)(2,1)S(1)}, u32[]{:S(2)}, u32[]{:S(2)}) collective-permute-start(bf16[1024,128]{1,0:T(8,128)(2,1)S(1)} %collective-permute-done.4.rest_3_), channel_id=1, source_target_pairs={{0,1},{1,0},{2,3},{3,2},{4,5},{5,4},{6,7},{7,6},{8,9},{9,8},{10,11... | collective-permute-start | bytes 786440 | tf_op jit(solution)/shard_map/ppermute | solution.py:44
  29.6 0.0 collective-permute-done.3.rest_2_
  29.6 0.0 collective-permute-start
  29.6 0.3 collective-permute-done.2.rest_1_
  29.9 0.3 collective-permute-start.7
  30.1 4.2 %collective-permute-done.1.rest_0_ = bf16[1024,128]{1,0:T(8,128)(2,1)S(1)} collective-permute-done((bf16[1024,128]{1,0:T(8,128)(2,1)S(1)}, bf16[1024,128]{1,0:T(8,128)(2,1)S(1)}, u32[]{:S(2)}, u32[]{:S(2)}) %collective-permute-start.1) | collective-permute-done | bytes 262176 | tf_op jit(solution)/shard_map/ppermute | solution.py:40
  34.4 0.0 collective-permute-start.6
  34.4 0.0 collective-permute-done.8.rest_7_
  34.4 0.5 collective-permute-start.5
  34.9 0.0 collective-permute-done.7.rest_6_
  34.9 1.0 %collective-permute-done.6.rest_5_ = bf16[1024,128]{1,0:T(8,128)(2,1)S(1)} collective-permute-done((bf16[1024,128]{1,0:T(8,128)(2,1)S(1)}, bf16[1024,128]{1,0:T(8,128)(2,1)S(1)}, u32[]{:S(2)}, u32[]{:S(2)}) %collective-permute-start.6) | collective-permute-done | bytes 262176 | tf_op jit(solution)/shard_map/ppermute | solution.py:44
  35.9 0.4 collective-permute-done.5.rest_4_
  36.3 0.0 collective-permute-done.rq_ref
  36.3 0.0 collective-permute-done.9.rest_9_
  36.3 0.0 copy-done
  36.3 0.0 copy-done.3
  36.3 0.0 copy-done.2
  36.3 0.0 copy-start.1
  36.3 1.0 %copy-done.1 = bf16[512,512]{1,0:T(8,128)(2,1)S(1)} copy-done((bf16[512,512]{1,0:T(8,128)(2,1)S(1)}, bf16[512,512]{1,0:T(8,128)(2,1)}, u32[]{:S(2)}) %copy-start.1) | copy-done | bytes 524312
  37.4 17.6 %attend.1 = (bf16[256,256]{1,0:T(8,128)(2,1)S(1)}, bf16[256,256]{1,0:T(8,128)(2,1)S(1)}, bf16[256,256]{1,0:T(8,128)(2,1)S(1)}, bf16[256,256]{1,0:T(8,128)(2,1)S(...) custom-call(s32[4]{0:T(128)S(1)} %copy-done.2, ...), custom_call_target="tpu_custom_call" | custom-call | flops 6000000000 | bytes 8388608 | tf_op jit(solution)/shard_map/attend/pallas_call | solution.py:162
  54.9 3.5 %collective-permute-start.10 = (bf16[256,256]{1,0:T(8,128)(2,1)S(1)}, bf16[256,256]{1,0:T(8,128)(2,1)S(1)}, u32[]{:S(2)}, u32[]{:S(2)}) collective-permute-start(bf16[256,256]{1,0:T(8,128)(2,1)S(1)} %get-tuple-element.14), channel_id=1, source_target_pairs={{0,2},{1,3},{2,4},{3,5},{4,6},{5,7},{6,0},{7,1},{8,10},{9,11},{10,... | collective-permute-start | bytes 393224 | tf_op jit(solution)/shard_map/ppermute | solution.py:53
  58.4 4.5 %collective-permute-start.11 = (bf16[256,256]{1,0:T(8,128)(2,1)S(1)}, bf16[256,256]{1,0:T(8,128)(2,1)S(1)}, u32[]{:S(2)}, u32[]{:S(2)}) collective-permute-start(bf16[256,256]{1,0:T(8,128)(2,1)S(1)} %get-tuple-element.15), channel_id=1, source_target_pairs={{0,4},{1,5},{2,6},{3,7},{4,0},{5,1},{6,2},{7,3},{8,12},{9,13},{10,... | collective-permute-start | bytes 393224 | tf_op jit(solution)/shard_map/ppermute | solution.py:53
  62.9 2.7 %collective-permute-start.12 = (bf16[256,256]{1,0:T(8,128)(2,1)S(1)}, bf16[256,256]{1,0:T(8,128)(2,1)S(1)}, u32[]{:S(2)}, u32[]{:S(2)}) collective-permute-start(bf16[256,256]{1,0:T(8,128)(2,1)S(1)} %get-tuple-element.16), channel_id=1, source_target_pairs={{0,6},{1,7},{2,0},{3,1},{4,2},{5,3},{6,4},{7,5},{8,14},{9,15},{10,... | collective-permute-start | bytes 393224 | tf_op jit(solution)/shard_map/ppermute | solution.py:53
  65.6 0.0 collective-permute-start.13
  65.6 0.4 collective-permute-start.14
  66.0 6.7 %collective-permute-done.10 = bf16[256,256]{1,0:T(8,128)(2,1)S(1)} collective-permute-done((bf16[256,256]{1,0:T(8,128)(2,1)S(1)}, bf16[256,256]{1,0:T(8,128)(2,1)S(1)}, u32[]{:S(2)}, u32[]{:S(2)}) %collective-permute-start.10) | collective-permute-done | bytes 131104 | tf_op jit(solution)/shard_map/ppermute | solution.py:53
  72.6 4.8 %collective-permute-start.15 = (bf16[256,256]{1,0:T(8,128)(2,1)S(1)}, bf16[256,256]{1,0:T(8,128)(2,1)S(1)}, u32[]{:S(2)}, u32[]{:S(2)}) collective-permute-start(bf16[256,256]{1,0:T(8,128)(2,1)S(1)} %get-tuple-element.19), channel_id=1, source_target_pairs={{0,5},{1,4},{2,7},{3,6},{4,1},{5,0},{6,3},{7,2},{8,13},{9,12},{10,... | collective-permute-start | bytes 393224 | tf_op jit(solution)/shard_map/ppermute | solution.py:53
  77.5 0.0 collective-permute-done.11
  77.5 0.0 collective-permute-start.16
  77.5 0.0 collective-permute-done.12
  77.5 0.1 add_convert_fusion.1
  77.6 0.0 collective-permute-done.13
  77.6 1.0 %collective-permute-done.14 = bf16[256,256]{1,0:T(8,128)(2,1)S(1)} collective-permute-done((bf16[256,256]{1,0:T(8,128)(2,1)S(1)}, bf16[256,256]{1,0:T(8,128)(2,1)S(1)}, u32[]{:S(2)}, u32[]{:S(2)}) %collective-permute-start.14) | collective-permute-done | bytes 131104 | tf_op jit(solution)/shard_map/ppermute | solution.py:53
  78.6 6.7 %collective-permute-done.15 = bf16[256,256]{1,0:T(8,128)(2,1)S(1)} collective-permute-done((bf16[256,256]{1,0:T(8,128)(2,1)S(1)}, bf16[256,256]{1,0:T(8,128)(2,1)S(1)}, u32[]{:S(2)}, u32[]{:S(2)}) %collective-permute-start.15) | collective-permute-done | bytes 131104 | tf_op jit(solution)/shard_map/ppermute | solution.py:53
  85.3 3.8 %collective-permute-done.16 = bf16[256,256]{1,0:T(8,128)(2,1)S(1)} collective-permute-done((bf16[256,256]{1,0:T(8,128)(2,1)S(1)}, bf16[256,256]{1,0:T(8,128)(2,1)S(1)}, u32[]{:S(2)}, u32[]{:S(2)}) %collective-permute-start.16) | collective-permute-done | bytes 131104 | tf_op jit(solution)/shard_map/ppermute | solution.py:53
  89.1 0.1 add_convert_fusion
  89.2 0.8 maximum_select_fusion
  (3 shorter events, 0.1 us)
Async XLA Ops:
  0.0 36.3 %copy-start = (bf16[512,2048]{1,0:T(8,128)(2,1)S(1)}, bf16[512,2048]{1,0:T(8,128)(2,1)}, u32[]{:S(2)}) copy-start(bf16[512,2048]{1,0:T(8,128)(2,1)} %rest_8_.1) | copy-start | bytes 6291460
  0.0 36.3 %copy-start.3 = (s32[1,35]{1,0:T(1,128)S(1)}, s32[1,35]{1,0:T(1,128)}, u32[]{:S(2)}) copy-start(s32[1,35]{1,0:T(1,128)} %list_ref.1) | copy-start | bytes 424
  0.0 36.3 %copy-start.2 = (s32[4]{0:T(128)S(1)}, s32[4]{0:T(128)}, u32[]{:S(2)}) copy-start(s32[4]{0:T(128)} %doc_ref.1) | copy-start | bytes 52
  0.0 36.3 %collective-permute-start.9 = (bf16[512,2048]{1,0:T(8,128)(2,1)}, bf16[512,2048]{1,0:T(8,128)(2,1)}, u32[]{:S(2)}, u32[]{:S(2)}) collective-permute-start(bf16[512,2048]{1,0:T(8,128)(2,1)} %rest_8_.1), channel_id=1, source_target_pairs={{0,1},{1,0},{2,3},{3,2},{4,5},{5,4},{6,7},{7,6},{8,9},{9,8},{10,11... | collective-permute-start | bytes 6291464 | tf_op jit(solution)/shard_map/ppermute | solution.py:44
  2.1 14.7 %collective-permute-start.4 = (bf16[1024,128]{1,0:T(8,128)(2,1)S(1)}, bf16[1024,128]{1,0:T(8,128)(2,1)S(1)}, u32[]{:S(2)}, u32[]{:S(2)}) collective-permute-start(bf16[1024,128]{1,0:T(8,128)(2,1)S(1)} %pad_maximum_fusion.own_ref), channel_id=1, source_target_pairs={{0,32},{1,65},{2,34},{3,67},{4,36},{5,69},{6,38},{7,71},{8,40},{9,... | collective-permute-start | bytes 786440 | tf_op jit(solution)/shard_map/ppermute | solution.py:40
  5.6 24.0 %collective-permute-start.3 = (bf16[1024,128]{1,0:T(8,128)(2,1)S(1)}, bf16[1024,128]{1,0:T(8,128)(2,1)S(1)}, u32[]{:S(2)}, u32[]{:S(2)}) collective-permute-start(bf16[1024,128]{1,0:T(8,128)(2,1)S(1)} %pad_maximum_fusion.own_ref), channel_id=1, source_target_pairs={{0,24},{1,57},{2,26},{3,59},{4,28},{5,61},{6,30},{7,63},{8,32},{9,... | collective-permute-start | bytes 786440 | tf_op jit(solution)/shard_map/ppermute | solution.py:40
  10.3 19.6 %collective-permute-start.2 = (bf16[1024,128]{1,0:T(8,128)(2,1)S(1)}, bf16[1024,128]{1,0:T(8,128)(2,1)S(1)}, u32[]{:S(2)}, u32[]{:S(2)}) collective-permute-start(bf16[1024,128]{1,0:T(8,128)(2,1)S(1)} %pad_maximum_fusion.own_ref), channel_id=1, source_target_pairs={{0,16},{1,49},{2,18},{3,51},{4,20},{5,53},{6,22},{7,55},{8,24},{9,... | collective-permute-start | bytes 786440 | tf_op jit(solution)/shard_map/ppermute | solution.py:40
  14.0 20.4 %collective-permute-start.1 = (bf16[1024,128]{1,0:T(8,128)(2,1)S(1)}, bf16[1024,128]{1,0:T(8,128)(2,1)S(1)}, u32[]{:S(2)}, u32[]{:S(2)}) collective-permute-start(bf16[1024,128]{1,0:T(8,128)(2,1)S(1)} %pad_maximum_fusion.own_ref), channel_id=1, source_target_pairs={{0,8},{1,41},{2,10},{3,43},{4,12},{5,45},{6,14},{7,47},{8,16},{9,4... | collective-permute-start | bytes 786440 | tf_op jit(solution)/shard_map/ppermute | solution.py:40
  16.8 17.6 %collective-permute-start.8 = (bf16[1024,128]{1,0:T(8,128)(2,1)S(1)}, bf16[1024,128]{1,0:T(8,128)(2,1)S(1)}, u32[]{:S(2)}, u32[]{:S(2)}) collective-permute-start(bf16[1024,128]{1,0:T(8,128)(2,1)S(1)} %collective-permute-done.4.rest_3_), channel_id=1, source_target_pairs={{0,1},{1,0},{2,3},{3,2},{4,5},{5,4},{6,7},{7,6},{8,9},{9,8},{10,11... | collective-permute-start | bytes 786440 | tf_op jit(solution)/shard_map/ppermute | solution.py:44
  29.6 6.7 %collective-permute-start = (bf16[512,512]{1,0:T(8,128)(2,1)}, bf16[512,512]{1,0:T(8,128)(2,1)S(1)}, u32[]{:S(2)}, u32[]{:S(2)}) collective-permute-start(bf16[512,512]{1,0:T(8,128)(2,1)} %q_ref.1), channel_id=1, source_target_pairs={{0,1},{1,0},{2,3},{3,2},{4,5},{5,4},{6,7},{7,6},{8,9},{9,8},{10,11... | collective-permute-start | bytes 1572872 | tf_op jit(solution)/shard_map/ppermute | solution.py:44
  29.9 5.0 %collective-permute-start.7 = (bf16[1024,128]{1,0:T(8,128)(2,1)S(1)}, bf16[1024,128]{1,0:T(8,128)(2,1)S(1)}, u32[]{:S(2)}, u32[]{:S(2)}) collective-permute-start(bf16[1024,128]{1,0:T(8,128)(2,1)S(1)} %collective-permute-done.3.rest_2_), channel_id=1, source_target_pairs={{0,1},{1,0},{2,3},{3,2},{4,5},{5,4},{6,7},{7,6},{8,9},{9,8},{10,11... | collective-permute-start | bytes 786440 | tf_op jit(solution)/shard_map/ppermute | solution.py:44
  34.4 1.5 %collective-permute-start.6 = (bf16[1024,128]{1,0:T(8,128)(2,1)S(1)}, bf16[1024,128]{1,0:T(8,128)(2,1)S(1)}, u32[]{:S(2)}, u32[]{:S(2)}) collective-permute-start(bf16[1024,128]{1,0:T(8,128)(2,1)S(1)} %collective-permute-done.2.rest_1_), channel_id=1, source_target_pairs={{0,1},{1,0},{2,3},{3,2},{4,5},{5,4},{6,7},{7,6},{8,9},{9,8},{10,11... | collective-permute-start | bytes 786440 | tf_op jit(solution)/shard_map/ppermute | solution.py:44
  34.4 1.9 %collective-permute-start.5 = (bf16[1024,128]{1,0:T(8,128)(2,1)S(1)}, bf16[1024,128]{1,0:T(8,128)(2,1)S(1)}, u32[]{:S(2)}, u32[]{:S(2)}) collective-permute-start(bf16[1024,128]{1,0:T(8,128)(2,1)S(1)} %collective-permute-done.1.rest_0_), channel_id=1, source_target_pairs={{0,1},{1,0},{2,3},{3,2},{4,5},{5,4},{6,7},{7,6},{8,9},{9,8},{10,11... | collective-permute-start | bytes 786440 | tf_op jit(solution)/shard_map/ppermute | solution.py:44
  36.3 1.0 %copy-start.1 = (bf16[512,512]{1,0:T(8,128)(2,1)S(1)}, bf16[512,512]{1,0:T(8,128)(2,1)}, u32[]{:S(2)}) copy-start(bf16[512,512]{1,0:T(8,128)(2,1)} %q_ref.1) | copy-start | bytes 1572868
  54.9 17.7 %collective-permute-start.10 = (bf16[256,256]{1,0:T(8,128)(2,1)S(1)}, bf16[256,256]{1,0:T(8,128)(2,1)S(1)}, u32[]{:S(2)}, u32[]{:S(2)}) collective-permute-start(bf16[256,256]{1,0:T(8,128)(2,1)S(1)} %get-tuple-element.14), channel_id=1, source_target_pairs={{0,2},{1,3},{2,4},{3,5},{4,6},{5,7},{6,0},{7,1},{8,10},{9,11},{10,... | collective-permute-start | bytes 393224 | tf_op jit(solution)/shard_map/ppermute | solution.py:53
  58.4 19.0 %collective-permute-start.11 = (bf16[256,256]{1,0:T(8,128)(2,1)S(1)}, bf16[256,256]{1,0:T(8,128)(2,1)S(1)}, u32[]{:S(2)}, u32[]{:S(2)}) collective-permute-start(bf16[256,256]{1,0:T(8,128)(2,1)S(1)} %get-tuple-element.15), channel_id=1, source_target_pairs={{0,4},{1,5},{2,6},{3,7},{4,0},{5,1},{6,2},{7,3},{8,12},{9,13},{10,... | collective-permute-start | bytes 393224 | tf_op jit(solution)/shard_map/ppermute | solution.py:53
  62.9 14.6 %collective-permute-start.12 = (bf16[256,256]{1,0:T(8,128)(2,1)S(1)}, bf16[256,256]{1,0:T(8,128)(2,1)S(1)}, u32[]{:S(2)}, u32[]{:S(2)}) collective-permute-start(bf16[256,256]{1,0:T(8,128)(2,1)S(1)} %get-tuple-element.16), channel_id=1, source_target_pairs={{0,6},{1,7},{2,0},{3,1},{4,2},{5,3},{6,4},{7,5},{8,14},{9,15},{10,... | collective-permute-start | bytes 393224 | tf_op jit(solution)/shard_map/ppermute | solution.py:53
  65.6 12.0 %collective-permute-start.13 = (bf16[256,256]{1,0:T(8,128)(2,1)S(1)}, bf16[256,256]{1,0:T(8,128)(2,1)S(1)}, u32[]{:S(2)}, u32[]{:S(2)}) collective-permute-start(bf16[256,256]{1,0:T(8,128)(2,1)S(1)} %get-tuple-element.17), channel_id=1, source_target_pairs={{0,1},{1,0},{2,3},{3,2},{4,5},{5,4},{6,7},{7,6},{8,9},{9,8},{10,11... | collective-permute-start | bytes 393224 | tf_op jit(solution)/shard_map/ppermute | solution.py:53
  65.6 13.0 %collective-permute-start.14 = (bf16[256,256]{1,0:T(8,128)(2,1)S(1)}, bf16[256,256]{1,0:T(8,128)(2,1)S(1)}, u32[]{:S(2)}, u32[]{:S(2)}) collective-permute-start(bf16[256,256]{1,0:T(8,128)(2,1)S(1)} %get-tuple-element.18), channel_id=1, source_target_pairs={{0,3},{1,2},{2,5},{3,4},{4,7},{5,6},{6,1},{7,0},{8,11},{9,10},{10,... | collective-permute-start | bytes 393224 | tf_op jit(solution)/shard_map/ppermute | solution.py:53
  72.6 12.6 %collective-permute-start.15 = (bf16[256,256]{1,0:T(8,128)(2,1)S(1)}, bf16[256,256]{1,0:T(8,128)(2,1)S(1)}, u32[]{:S(2)}, u32[]{:S(2)}) collective-permute-start(bf16[256,256]{1,0:T(8,128)(2,1)S(1)} %get-tuple-element.19), channel_id=1, source_target_pairs={{0,5},{1,4},{2,7},{3,6},{4,1},{5,0},{6,3},{7,2},{8,13},{9,12},{10,... | collective-permute-start | bytes 393224 | tf_op jit(solution)/shard_map/ppermute | solution.py:53
  77.5 11.6 %collective-permute-start.16 = (bf16[256,256]{1,0:T(8,128)(2,1)S(1)}, bf16[256,256]{1,0:T(8,128)(2,1)S(1)}, u32[]{:S(2)}, u32[]{:S(2)}) collective-permute-start(bf16[256,256]{1,0:T(8,128)(2,1)S(1)} %get-tuple-element.20), channel_id=1, source_target_pairs={{0,7},{1,6},{2,1},{3,0},{4,3},{5,2},{6,5},{7,4},{8,15},{9,14},{10,... | collective-permute-start | bytes 393224 | tf_op jit(solution)/shard_map/ppermute | solution.py:53

commit v2 on v0

v2 whole, which is shorter than its diff:
```python
import functools
import math

import jax
import jax.numpy as jnp
from jax import lax
from jax.experimental import pallas as pl
from jax.experimental.pallas import tpu as pltpu
from jax.sharding import PartitionSpec as P

HEAD_WIDTH = 128
BLK = 128
DOC_BLOCKS = 32
REACH = 8
SHARD = 512
HALF = 256
PIECE = 256
NEG = -1e30
EXP_SCALE = math.log2(math.e) / math.sqrt(HEAD_WIDTH)
AXES = ("ctx", "head")
X_CHIPS = 4
GRANT = 40 * 2**20


def ctx_head_pairs(n_ctx, n_head, route):
    pairs = []
    for c in range(n_ctx):
        for h in range(n_head):
            target = route(c, h)
            if target is not None:
                pairs.append((c * n_head + h, target[0] * n_head + target[1]))
    return pairs


def send(block, n_ctx, n_head, route):
    return lax.ppermute(block, AXES, ctx_head_pairs(n_ctx, n_head, route))


def to_later_rows(n_ctx):
    def route(c, h):
        d = c + 4 + 4 * (h % 2)
        return (d, h) if d < n_ctx else None

    return route


def turned(c, by):
    return c - c % X_CHIPS + (c + by) % X_CHIPS


def beside(c, h):
    return (turned(c, 1 if h % 2 == 0 else 3), h)


def across(c, h):
    return (turned(c, 2), h)


def other_core(c, h):
    return (c, h ^ 1)


def along_z(n_head):
    return lambda c, h: (c, (h + (2 if h % 2 == 0 else -2)) % n_head)


def dot_t(a, b):
    return lax.dot_general(
        a, b, (((1,), (1,)), ((), ())), preferred_element_type=jnp.float32
    )


def position():
    head = lax.axis_index("head")
    return lax.axis_index("ctx"), lax.div(head, 2), lax.rem(head, 2)


class Copies:
    def __init__(self, sem):
        self.sem, self.started = sem, []

    def start(self, src, dst):
        c = pltpu.make_async_copy(src, dst, self.sem.at[len(self.started)])
        c.start()
        self.started.append(c)

    def wait(self, first=0, last=None):
        for c in self.started[first:last]:
            c.wait()


def last_listed(list_ref):
    last = list_ref[0, 0]
    for i in range(1, list_ref.shape[1]):
        last = jnp.maximum(last, list_ref[0, i])
    return last


def block_range(doc_ref, list_ref, list_last, ctx, local):
    lo = jnp.maximum(doc_ref[local], list_ref[0, 0])
    hi = jnp.minimum(ctx * (SHARD // BLK) + local, list_last)
    return lo, hi


def write_bias(bias, ctx, distances, lo, hi):
    for j, d in enumerate(distances):
        block = (ctx - d) * (SHARD // BLK) + (
            lax.broadcasted_iota(jnp.int32, (bias.shape[0], SHARD), 1) // BLK
        )
        bias[:, j * SHARD : (j + 1) * SHARD] = jnp.where(
            (block >= lo) & (block <= hi), 0.0, NEG
        )


def load_shard(copies, ref, first, kx, vx, row):
    copies.start(ref.at[pl.ds(first, SHARD)], kx.at[pl.ds(row, SHARD)])
    copies.start(
        ref.at[pl.ds(first + SHARD, SHARD)],
        vx.at[pl.ds(row, SHARD), pl.ds(0, HEAD_WIDTH)],
    )


def softmax_tile(q, k, v, mask, m, acc):
    s = dot_t(q, k) + mask
    top = jnp.max(s, axis=1, keepdims=True)
    m_new = top if m is None else jnp.maximum(m, top)
    p = jnp.exp2((s - m_new) * EXP_SCALE).astype(jnp.bfloat16)
    pv = jnp.dot(p, v, preferred_element_type=jnp.float32)
    if m is not None:
        pv = acc * jnp.exp2((m - m_new) * EXP_SCALE) + pv
    return m_new, pv


def head_columns(g):
    return slice(g * HEAD_WIDTH, (g + 1) * HEAD_WIDTH)


def turn_distances(core):
    return [jnp.where(core == 0, a, b) for a, b in ((1, 3), (5, 7), (2, 6))]


def load_queries(copies, q_ref, rq_ref, row, rows, qs):
    at = pl.multiple_of(row, BLK)
    copies.start(q_ref.at[pl.ds(at, rows)], qs.at[:, pl.ds(0, 512)])
    copies.start(rq_ref.at[pl.ds(at, rows)], qs.at[:, pl.ds(512, 512)])


def near_kernel(doc_ref, list_ref, q_ref, rq_ref, own, mine, theirs, *rest):
    acc_ref, ml_ref, kx, vx, qs, mask, sem = rest
    ctx, z, core = position()
    copies = Copies(sem)
    load_queries(copies, q_ref, rq_ref, core * HALF, HALF, qs)
    load_shard(copies, own, 0, kx, vx, 0)
    load_shard(copies, mine, 0, kx, vx, pl.multiple_of((1 + core) * SHARD, SHARD))
    load_shard(copies, theirs, 0, kx, vx, pl.multiple_of((2 - core) * SHARD, SHARD))
    vx[:, HEAD_WIDTH:] = jnp.ones((vx.shape[0], HEAD_WIDTH), jnp.bfloat16)
    lane = lax.broadcasted_iota(jnp.int32, (BLK, HEAD_WIDTH), 1)
    list_last = last_listed(list_ref)

    def write_mask(ii):
        local = core * 2 + ii
        lo, hi = block_range(doc_ref, list_ref, list_last, ctx, local)
        write_bias(mask, ctx, (0, 4, 8), lo, hi)
        col = lax.broadcasted_iota(jnp.int32, (BLK, SHARD), 1)
        at = lax.broadcasted_iota(jnp.int32, (BLK, SHARD), 0) + local * BLK
        mask[:, :SHARD] = jnp.where(col <= at, mask[:, :SHARD], NEG)

    def block(ii, carry):
        rows = pl.ds(pl.multiple_of(ii * BLK, BLK), BLK)
        ml = jnp.zeros((BLK, HEAD_WIDTH), jnp.float32)
        for g in range(8):
            q = qs[rows, head_columns(g)]
            m, acc = softmax_tile(q, kx[...], vx[...], mask[...], None, None)
            acc_ref[rows, head_columns(g)] = acc[:, :HEAD_WIDTH]
            ml = jnp.where(lane == g, m, ml)
            ml = jnp.where(lane == 8 + g, acc[:, HEAD_WIDTH:], ml)
        ml_ref[rows, :] = ml

        @pl.when(ii == 0)
        def _():
            write_mask(1)

        return carry

    write_mask(0)
    copies.wait()
    lax.fori_loop(0, 2, block, 0)


def joined(acc_ref, ml_ref, rows, g):
    l_in = jnp.broadcast_to(ml_ref[rows, 8 + g : 9 + g], (BLK, HEAD_WIDTH))
    acc = jnp.concatenate([acc_ref[rows, head_columns(g)], l_in], axis=1)
    return ml_ref[rows, g : g + 1], acc


def far_kernel(doc_ref, list_ref, q_ref, rq_ref, *rest):
    turns, (acc_in, ml_in, ho) = rest[:4], rest[4:7]
    kx, vx, qs, bias, acc_s, ml_s, sem = rest[7:]
    ctx, z, core = position()
    copies = Copies(sem)
    for i in range(2):
        at = 3 * i * SHARD
        load_shard(copies, turns[2 * i], 0, kx, vx, at)
        load_shard(copies, turns[2 * i], 2 * SHARD, kx, vx, at + SHARD)
        load_shard(copies, turns[2 * i + 1], 0, kx, vx, at + 2 * SHARD)
    load_queries(copies, q_ref, rq_ref, core * HALF, HALF, qs)
    copies.start(acc_in, acc_s)
    copies.start(ml_in, ml_s)
    vx[:, HEAD_WIDTH:] = jnp.ones((vx.shape[0], HEAD_WIDTH), jnp.bfloat16)
    distances = turn_distances(core) + turn_distances(1 - core)
    list_last = last_listed(list_ref)
    for ii in range(2):
        lo, hi = block_range(doc_ref, list_ref, list_last, ctx, core * 2 + ii)
        write_bias(bias.at[ii], ctx, distances, lo, hi)
    copies.wait()

    def block(ii, carry):
        rows = pl.ds(pl.multiple_of(ii * BLK, BLK), BLK)
        for g in range(8):
            q = qs[rows, head_columns(g)]
            m, acc = joined(acc_s, ml_s, rows, g)
            _, acc = softmax_tile(q, kx[...], vx[...], bias[ii, 0:1, :], m, acc)
            o = acc[:, :HEAD_WIDTH] / acc[:, HEAD_WIDTH:]
            ho[rows, head_columns(g)] = o.astype(jnp.bfloat16)
        return carry

    lax.fori_loop(0, 2, block, 0)

def project_kernel(ho_ref, got_ref, w_ref, rw_ref, *rest):
    outs = rest[:4]
    ho, ws, sem = rest[4:]
    ctx, z, core = position()
    copies = Copies(sem)
    dz = jnp.where(core == 0, 1, 3)
    wanted = ((2, core), (dz, 1 - core), (dz, core), (0, core))
    mine = pl.ds(pl.multiple_of(core * HALF, HALF), HALF)
    theirs = pl.ds(pl.multiple_of((1 - core) * HALF, HALF), HALF)
    copies.start(ho_ref, ho.at[mine])
    copies.start(got_ref.at[:, pl.ds(0, 512)], ho.at[theirs, pl.ds(512, 512)])
    copies.start(got_ref.at[:, pl.ds(512, 512)], ho.at[theirs, pl.ds(0, 512)])
    for i, (away, part) in enumerate(wanted):
        target = lax.rem(z + away, 4) * 2 + part
        col = pl.ds(pl.multiple_of(target * PIECE, PIECE), PIECE)
        copies.start(w_ref.at[:, col], ws.at[i, pl.ds(0, 512)])
        copies.start(rw_ref.at[:, col], ws.at[i, pl.ds(512, 512)])
    copies.wait(0, 3)
    for i, out in enumerate(outs):
        copies.wait(3 + 2 * i, 5 + 2 * i)
        out[...] = jnp.dot(
            ho[...], ws[i], preferred_element_type=jnp.float32
        ).astype(jnp.bfloat16)


SMEM = pl.BlockSpec(memory_space=pltpu.SMEM)
ANY = pl.BlockSpec(memory_space=pl.ANY)
VMEM = pl.BlockSpec(memory_space=pltpu.VMEM)


def key_scratch(keys):
    return [
        pltpu.VMEM((keys, HEAD_WIDTH), jnp.bfloat16),
        pltpu.VMEM((keys, 2 * HEAD_WIDTH), jnp.bfloat16),
    ]


STATE = [
    jax.ShapeDtypeStruct((HALF, 8 * HEAD_WIDTH), jnp.float32),
    jax.ShapeDtypeStruct((HALF, HEAD_WIDTH), jnp.float32),
]


def call(kernel, name, out_shape, scratch, keys, rows, args):
    return pl.pallas_call(
        kernel,
        out_shape=out_shape,
        in_specs=[SMEM, SMEM] + [ANY] * (len(args) - 2),
        out_specs=[VMEM] * len(out_shape),
        scratch_shapes=scratch,
        compiler_params=pltpu.CompilerParams(vmem_limit_bytes=GRANT),
        cost_estimate=pl.CostEstimate(
            flops=8 * rows * keys * 2 * HEAD_WIDTH * 2,
            bytes_accessed=4 * 2**20,
            transcendentals=8 * rows * keys,
        ),
        name=name,
    )(*args)


def near(*args):
    scratch = key_scratch(3 * SHARD) + [
        pltpu.VMEM((HALF, 1024), jnp.bfloat16),
        pltpu.VMEM((BLK, 3 * SHARD), jnp.float32),
        pltpu.SemaphoreType.DMA((8,)),
    ]
    return call(near_kernel, "near", STATE, scratch, 3 * SHARD, HALF, args)


def far(*args):
    scratch = key_scratch(6 * SHARD) + [
        pltpu.VMEM((HALF, 1024), jnp.bfloat16),
        pltpu.VMEM((2, 8, 6 * SHARD), jnp.float32),
        pltpu.VMEM((HALF, 1024), jnp.float32),
        pltpu.VMEM((HALF, HEAD_WIDTH), jnp.float32),
        pltpu.SemaphoreType.DMA((16,)),
    ]
    out = jax.ShapeDtypeStruct((HALF, 1024), jnp.bfloat16)
    return call(far_kernel, "far", [out], scratch, 6 * SHARD, HALF, args)[0]


def project(*args):
    out = jax.ShapeDtypeStruct((SHARD, PIECE), jnp.bfloat16)
    return pl.pallas_call(
        project_kernel,
        out_shape=[out] * 4,
        in_specs=[ANY] * 4,
        out_specs=[VMEM] * 4,
        scratch_shapes=[
            pltpu.VMEM((SHARD, 1024), jnp.bfloat16),
            pltpu.VMEM((4, 1024, PIECE), jnp.bfloat16),
            pltpu.SemaphoreType.DMA((11,)),
        ],
        compiler_params=pltpu.CompilerParams(vmem_limit_bytes=GRANT),
        cost_estimate=pl.CostEstimate(
            flops=10**9, bytes_accessed=4 * 2**20, transcendentals=0
        ),
        name="project",
    )(*args)


def f32_sum(*terms):
    return sum(t.astype(jnp.float32) for t in terms).astype(jnp.bfloat16)


def on_device(n_ctx, n_head, queries, key_rows, value_vectors, out_weight, doc_start, block_list):
    head = lax.axis_index("head")
    core = head % 2
    z = head // 2
    x = lax.axis_index("ctx") % X_CHIPS

    def go(block, route):
        return send(block, n_ctx, n_head, route)

    def pick(first, *arrays):
        return [jnp.where(first, a, b) for a, b in zip(arrays[:-1], arrays[1:])]

    own = jnp.concatenate(
        [
            lax.dynamic_index_in_dim(a, z, 1, keepdims=False)
            for a in (key_rows, value_vectors)
        ]
    )
    rq = go(queries, other_core)
    rw = go(out_weight, other_core)
    row_mine = go(own, to_later_rows(n_ctx))
    row_theirs = go(row_mine, other_core)
    four = jnp.where(core == 0, row_mine, row_theirs)
    eight = jnp.where(core == 0, row_theirs, row_mine)
    wraps = jnp.where(core == 0, x == X_CHIPS - 1, x >= 1)
    beside_load = jnp.concatenate(
        [jnp.where(wraps, four, own), jnp.where(wraps, eight, four)]
    )
    wraps = x >= X_CHIPS // 2
    across_load = jnp.where(
        core == 0, jnp.where(wraps, four, own), jnp.where(wraps, eight, four)
    )
    near_turn = go(beside_load, beside)
    far_turn = go(across_load, across)
    acc, ml = near(doc_start, block_list, queries, rq, own, row_mine, row_theirs)
    near_turn, far_turn, acc = lax.optimization_barrier((near_turn, far_turn, acc))
    turns = (
        near_turn, far_turn, go(near_turn, other_core), go(far_turn, other_core)
    )
    ho = far(doc_start, block_list, queries, rq, *turns, acc, ml)
    relay, plain, fwd, keep = project(ho, go(ho, other_core), out_weight, rw)
    came = go(relay, along_z(n_head))
    beyond = go(plain, along_z(n_head))
    summed = go(f32_sum(fwd, came), along_z(n_head))
    return f32_sum(keep, summed, go(beyond, other_core))


def solution(mesh):
    n_ctx, n_head = mesh.shape["ctx"], mesh.shape["head"]
    return jax.shard_map(
        functools.partial(on_device, n_ctx, n_head),
        mesh=mesh,
        in_specs=(
            P("ctx", "head"),
            P("ctx", None, None),
            P("ctx", None, None),
            P("head", None),
            P("ctx"),
            P("ctx", None),
        ),
        out_specs=P("ctx", "head"),
        check_vma=False,
    )
```

time: 212 us -> 82.1 us (0.39); the launches traced: 210 us -> 81.9 us
  waiting for transfers between devices: 121 us -> 35.3 us
  matrix products: 29.4 us -> 0 us
  Pallas kernels: 0 us -> 22.9 us
  between operations: 13.5 us -> 0.13 us
  local copies, waits for them, and re-layouts: 14.4 us -> 2.6 us
  other arithmetic: 14.3 us -> 3.06 us
    ppermute x8 -> x13, waiting for transfers between devices: 81.3 us -> 35.3 us  [send(): return lax.ppermute(block, AXES, ctx_head_pairs(n_ctx, n_head, route))]
    reduce_scatter x1 -> x0, waiting for transfers between devices: 39.2 us -> none  [on_device(): lax.psum_scatter(partial_value.astype(jnp.bfloat16), 'head', scatter_dime...]
    dot_general x19 -> x0, matrix products: 29.4 us -> none  [the longest x9 17.8 us: attend(): jnp.einsum('kgts,skd->kgtd', weights.astype(jnp.bfloat16), shard_piece[1]...]
    pallas_call x0 -> x3, Pallas kernels: none -> 22.9 us  [the longest x2 19 us: call(): pl.pallas_call(kernel, out_shape=out_shape, in_specs=[SMEM, SMEM] + [ANY]...]
    while x49 -> x0, local copies, waits for them, and re-layouts: 9.62 us -> none
    reduce_sum x9 -> x0, other arithmetic: 9.38 us -> none  [attend(): new_sum = run_sum * factor + jnp.sum(weights, axis=-1)]
    and x9 -> x0, other arithmetic: 2.8 us -> none  [attend(): (key_pos[None, :] <= query_pos[:, None]) & (key_block[None, :] >= query_d...]
    ppermute x8 -> x13, starting transfers between devices: 16.8 us -> 17.9 us  [send(): return lax.ppermute(block, AXES, ctx_head_pairs(n_ctx, n_head, route))]
  transfers between devices with their start and end apart: 9 -> 13, of which waited for: 9 -> 8; matrix products, arithmetic and copies ran while one was open for 2% -> 3% of each run, Pallas kernels for 0% -> 23%
where the time goes in v2:
time: 82.1 us; the launch traced here: 81.9 us
  waiting for transfers between devices  35.3 us (43%)
  Pallas kernels  22.9 us (28%)
  starting transfers between devices  17.9 us (22%)
  other arithmetic  3.06 us (4%)
  local copies, waits for them, and re-layouts  2.6 us (3%)
    ppermute x13, waiting for transfers between devices, send(): return lax.ppermute(block, AXES, ctx_head_pairs(n_ctx, n_head, route))  35.3 us
    pallas_call x2, Pallas kernels, call(): pl.pallas_call(kernel, out_shape=out_shape, in_specs=[SMEM, SMEM] + [ANY]...  19 us
    ppermute x13, starting transfers between devices, send(): return lax.ppermute(block, AXES, ctx_head_pairs(n_ctx, n_head, route))  17.9 us
    pallas_call x1, Pallas kernels, project(): pl.pallas_call(project_kernel, out_shape=[out] * 4, in_specs=[ANY] * 4, o...  3.93 us
    dynamic_slice x1, local copies, waits for them, and re-layouts, on_device(): lax.dynamic_index_in_dim(a, z, 1, keepdims=False)  1.89 us
  transfers between devices with their start and end apart: 13, of which 8 were waited for; matrix products, arithmetic and copies ran while one was open for 3% of the time, Pallas kernels for 23%

profile of v2, /device:TPU:32, one launch (start us, length us, event | category | flops | bytes accessed | tf_op | source)
XLA Modules:
  0.0 81.9 jit_solution(3194059406296259285)
XLA Ops:
  0.0 0.0 copy-start
  0.0 1.9 %constant_dynamic-slice_fusion = (bf16[512,1,128]{2,1,0:T(2,128)(2,1)S(1)}, bf16[512,1,128]{2,1,0:T(2,128)(2,1)S(1)}) fusion(bf16[512,4,128]{2,1,0:T(4,128)(2,1)} %param.8, s32[]{:T(128)S(6)} %select_n.66, bf16[512,4,128]{2,1,0:T(4,128)(2,1)} %param.7), kind=kLoop, calls=%fused_computation.11 | loop fusion | bytes 524292 | tf_op jit(solution)/shard_map/jit(dynamic_index_in_dim)/dynamic_slice | solution.py:348
  2.0 0.0 copy-start.4
  2.0 0.6 copy-done.4
  2.6 0.0 copy-start.1
  2.6 0.0 copy-start.2
  2.7 0.0 copy-start.3
  2.7 3.6 %collective-permute-start.1 = (bf16[1024,128]{1,0:T(8,128)(2,1)S(1)}, bf16[1024,128]{1,0:T(8,128)(2,1)S(1)}, u32[]{:S(2)}, u32[]{:S(2)}) collective-permute-start(bf16[1024,128]{1,0:T(8,128)(2,1)S(1)} %pad_maximum_fusion.1.own), channel_id=1, source_target_pairs={{0,32},{1,65},{2,34},{3,67},{4,36},{5,69},{6,38},{7,71},{8,40},{9,... | collective-permute-start | bytes 786440 | tf_op jit(solution)/shard_map/ppermute | solution.py:36
  6.3 9.6 %collective-permute-done.1.mine = bf16[1024,128]{1,0:T(8,128)(2,1)S(1)} collective-permute-done((bf16[1024,128]{1,0:T(8,128)(2,1)S(1)}, bf16[1024,128]{1,0:T(8,128)(2,1)S(1)}, u32[]{:S(2)}, u32[]{:S(2)}) %collective-permute-start.1) | collective-permute-done | bytes 262176 | tf_op jit(solution)/shard_map/ppermute | solution.py:36
  15.9 0.0 collective-permute-start.2
  15.9 0.5 collective-permute-start
  16.4 0.0 copy-done
  16.4 0.0 collective-permute-start.8
  16.4 1.4 %collective-permute-done.2.theirs = bf16[1024,128]{1,0:T(8,128)(2,1)S(1)} collective-permute-done((bf16[1024,128]{1,0:T(8,128)(2,1)S(1)}, bf16[1024,128]{1,0:T(8,128)(2,1)S(1)}, u32[]{:S(2)}, u32[]{:S(2)}) %collective-permute-start.2) | collective-permute-done | bytes 262176 | tf_op jit(solution)/shard_map/ppermute | solution.py:36
  17.7 1.1 %select_select_fusion = (bf16[1024,128]{1,0:T(8,128)(2,1)S(1)}, bf16[1024,128]{1,0:T(8,128)(2,1)S(1)}) fusion(pred[]{:T(512)S(6)} %ge.7, pred[]{:T(512)S(6)} %eq.12, bf16[1024,128]{1,0:T(8,128)(2,1)S(1)} %collective-permute-done.2.theirs, bf16[1024,128]{1,0:T(8,128)(2,1)S(1)} %collective-permute-done.1.mine, bf16[512,128]{1,0:T(8,128)(2,1)S(1)} %bitcast.7, ...), kind=kLoop, calls=%fused_computation.4 | loop fusion | flops 1179648 | bytes 1310722 | tf_op jit(solution)/shard_map/jit(_where)/select_n | solution.py:363
  18.8 1.1 %broadcast_select_fusion.3 = (bf16[1024,128]{1,0:T(8,128)(2,1)S(1)}, bf16[1024,128]{1,0:T(8,128)(2,1)S(1)}) fusion(bf16[1024,128]{1,0:T(8,128)(2,1)S(1)} %get-tuple-element.24, pred[]{:T(512)S(6)} %select_n.62, bf16[512,128]{1,0:T(8,128)(2,1)S(1)} %bitcast.8, bf16[512,128]{1,0:T(8,128)(2,1)} %bitcast.11, ...), kind=kLoop, calls=%fused_computation.8 | loop fusion | flops 917504 | bytes 1572866 | tf_op jit(solution)/shard_map/jit(_where)/select_n | solution.py:360
  19.9 1.6 %collective-permute-start.3 = (bf16[2048,128]{1,0:T(8,128)(2,1)S(1)}, bf16[2048,128]{1,0:T(8,128)(2,1)S(1)}, u32[]{:S(2)}, u32[]{:S(2)}) collective-permute-start(bf16[2048,128]{1,0:T(8,128)(2,1)S(1)} %pad_maximum_fusion), channel_id=1, source_target_pairs={{0,8},{1,25},{2,10},{3,27},{4,12},{5,29},{6,14},{7,31},{8,16},{9,1... | collective-permute-start | bytes 1572872 | tf_op jit(solution)/shard_map/ppermute | solution.py:36
  21.5 2.7 %collective-permute-start.4 = (bf16[1024,128]{1,0:T(8,128)(2,1)S(1)}, bf16[1024,128]{1,0:T(8,128)(2,1)S(1)}, u32[]{:S(2)}, u32[]{:S(2)}) collective-permute-start(bf16[1024,128]{1,0:T(8,128)(2,1)S(1)} %get-tuple-element.23), channel_id=1, source_target_pairs={{0,16},{1,17},{2,18},{3,19},{4,20},{5,21},{6,22},{7,23},{8,24},{9,... | collective-permute-start | bytes 786440 | tf_op jit(solution)/shard_map/ppermute | solution.py:36
  24.2 0.0 collective-permute-done.rq_ref
  24.2 0.0 copy-done.1
  24.2 0.0 copy-done.2
  24.2 0.0 copy-done.3
  24.3 6.7 %near.1 = (f32[256,1024]{1,0:T(8,128)S(1)}, f32[256,128]{1,0:T(8,128)S(1)}) custom-call(s32[4]{0:T(128)S(1)} %copy-done.2, s32[1,35]{1,0:T(1,128)S(1)} %copy-done.3, bf16[512,512]{1,0:T(8,128)(2,1)S(1)} %copy-done.1, bf16[512,512]{1,0:T(8,128)(2,1)} %collective-permute-done.rq_ref, bf16[1024,128]{1,0:T(8,128)(2,1)S(1)} %pad_maximum_fusion.1.own, ...), custom_call_target="tpu_custom_call" | custom-call | flops 1610612736 | bytes 4194304 | tf_op jit(solution)/shard_map/near/pallas_call | solution.py:273
  30.9 6.1 %collective-permute-done.4.rest_1_ = bf16[1024,128]{1,0:T(8,128)(2,1)S(1)} collective-permute-done((bf16[1024,128]{1,0:T(8,128)(2,1)S(1)}, bf16[1024,128]{1,0:T(8,128)(2,1)S(1)}, u32[]{:S(2)}, u32[]{:S(2)}) %collective-permute-start.4) | collective-permute-done | bytes 262176 | tf_op jit(solution)/shard_map/ppermute | solution.py:36
  37.0 0.0 collective-permute-done.3.rest_0_
  37.0 0.0 collective-permute-start.5
  37.0 0.5 collective-permute-start.6
  37.5 1.8 %collective-permute-done.6.rest_3_ = bf16[1024,128]{1,0:T(8,128)(2,1)S(1)} collective-permute-done((bf16[1024,128]{1,0:T(8,128)(2,1)S(1)}, bf16[1024,128]{1,0:T(8,128)(2,1)S(1)}, u32[]{:S(2)}, u32[]{:S(2)}) %collective-permute-start.6) | collective-permute-done | bytes 262176 | tf_op jit(solution)/shard_map/ppermute | solution.py:36
  39.3 0.0 collective-permute-done.5.rest_2_
  39.3 12.3 %far.1.ho_ref = bf16[256,1024]{1,0:T(8,128)(2,1)S(1)} custom-call(s32[4]{0:T(128)S(1)} %copy-done.2, s32[1,35]{1,0:T(1,128)S(1)} %copy-done.3, bf16[512,512]{1,0:T(8,128)(2,1)S(1)} %copy-done.1, bf16[512,512]{1,0:T(8,128)(2,1)} %collective-permute-done.rq_ref, bf16[2048,128]{1,0:T(8,128)(2,1)S(1)} %collective-permute-done.3.rest_0_, ...), custom_call_target="tpu_custom_call" | custom-call | flops 3221225472 | bytes 4194304 | tf_op jit(solution)/shard_map/far/pallas_call | solution.py:273
  51.7 0.2 collective-permute-start.7
  51.9 1.8 %collective-permute-done.7.got_ref = bf16[256,1024]{1,0:T(8,128)(2,1)S(1)} collective-permute-done((bf16[256,1024]{1,0:T(8,128)(2,1)S(1)}, bf16[256,1024]{1,0:T(8,128)(2,1)S(1)}, u32[]{:S(2)}, u32[]{:S(2)}) %collective-permute-start.7) | collective-permute-done | bytes 524320 | tf_op jit(solution)/shard_map/ppermute | solution.py:36
  53.7 0.0 collective-permute-done.8.rw_ref
  53.7 3.9 %project.1 = (bf16[512,256]{1,0:T(8,128)(2,1)S(1)}, bf16[512,256]{1,0:T(8,128)(2,1)S(1)}, bf16[512,256]{1,0:T(8,128)(2,1)S(1)}, bf16[512,256]{1,0:T(8,128)(2,1)S(1)}) custom-call(bf16[256,1024]{1,0:T(8,128)(2,1)S(1)} %far.1.ho_ref, bf16[256,1024]{1,0:T(8,128)(2,1)S(1)} %collective-permute-done.7.got_ref, bf16[512,2048]{1,0:T(8,128)(2,1)S(1)} %copy-done, ...), custom_call_target="tpu_custom_call" | custom-call | flops 1000000000 | bytes 4194304 | tf_op jit(solution)/shard_map/project/pallas_call | solution.py:312
  57.6 3.3 %collective-permute-start.9 = (bf16[512,256]{1,0:T(8,128)(2,1)S(1)}, bf16[512,256]{1,0:T(8,128)(2,1)S(1)}, u32[]{:S(2)}, u32[]{:S(2)}) collective-permute-start(bf16[512,256]{1,0:T(8,128)(2,1)S(1)} %get-tuple-element.21), channel_id=1, source_target_pairs={{0,2},{1,7},{2,4},{3,1},{4,6},{5,3},{6,0},{7,5},{8,10},{9,15},{10,... | collective-permute-start | bytes 786440 | tf_op jit(solution)/shard_map/ppermute | solution.py:36
  60.9 3.6 %collective-permute-start.11 = (bf16[512,256]{1,0:T(8,128)(2,1)S(1)}, bf16[512,256]{1,0:T(8,128)(2,1)S(1)}, u32[]{:S(2)}, u32[]{:S(2)}) collective-permute-start(bf16[512,256]{1,0:T(8,128)(2,1)S(1)} %get-tuple-element.22), channel_id=1, source_target_pairs={{0,2},{1,7},{2,4},{3,1},{4,6},{5,3},{6,0},{7,5},{8,10},{9,15},{10,... | collective-permute-start | bytes 786440 | tf_op jit(solution)/shard_map/ppermute | solution.py:36
  64.5 5.9 %collective-permute-done.9 = bf16[512,256]{1,0:T(8,128)(2,1)S(1)} collective-permute-done((bf16[512,256]{1,0:T(8,128)(2,1)S(1)}, bf16[512,256]{1,0:T(8,128)(2,1)S(1)}, u32[]{:S(2)}, u32[]{:S(2)}) %collective-permute-start.9) | collective-permute-done | bytes 262176 | tf_op jit(solution)/shard_map/ppermute | solution.py:36
  70.4 0.1 add_convert_fusion.1
  70.5 0.8 collective-permute-start.10
  71.3 2.0 %collective-permute-done.11 = bf16[512,256]{1,0:T(8,128)(2,1)S(1)} collective-permute-done((bf16[512,256]{1,0:T(8,128)(2,1)S(1)}, bf16[512,256]{1,0:T(8,128)(2,1)S(1)}, u32[]{:S(2)}, u32[]{:S(2)}) %collective-permute-start.11) | collective-permute-done | bytes 262176 | tf_op jit(solution)/shard_map/ppermute | solution.py:36
  73.3 1.1 %collective-permute-start.12 = (bf16[512,256]{1,0:T(8,128)(2,1)S(1)}, bf16[512,256]{1,0:T(8,128)(2,1)S(1)}, u32[]{:S(2)}, u32[]{:S(2)}) collective-permute-start(bf16[512,256]{1,0:T(8,128)(2,1)S(1)} %collective-permute-done.11), channel_id=1, source_target_pairs={{0,1},{1,0},{2,3},{3,2},{4,5},{5,4},{6,7},{7,6},{8,9},{9,8},{10,11... | collective-permute-start | bytes 786440 | tf_op jit(solution)/shard_map/ppermute | solution.py:36
  74.3 6.8 %collective-permute-done.10 = bf16[512,256]{1,0:T(8,128)(2,1)S(1)} collective-permute-done((bf16[512,256]{1,0:T(8,128)(2,1)S(1)}, bf16[512,256]{1,0:T(8,128)(2,1)S(1)}, u32[]{:S(2)}, u32[]{:S(2)}) %collective-permute-start.10) | collective-permute-done | bytes 262176 | tf_op jit(solution)/shard_map/ppermute | solution.py:36
  81.1 0.0 collective-permute-done.12
  81.1 0.8 add_convert_fusion
  (4 shorter events, 0.1 us)
Async XLA Ops:
  0.0 16.4 %copy-start = (bf16[512,2048]{1,0:T(8,128)(2,1)S(1)}, bf16[512,2048]{1,0:T(8,128)(2,1)}, u32[]{:S(2)}) copy-start(bf16[512,2048]{1,0:T(8,128)(2,1)} %w_ref.1) | copy-start | bytes 6291460
  2.0 0.7 copy-start.4
  2.6 21.6 %copy-start.1 = (bf16[512,512]{1,0:T(8,128)(2,1)S(1)}, bf16[512,512]{1,0:T(8,128)(2,1)}, u32[]{:S(2)}) copy-start(bf16[512,512]{1,0:T(8,128)(2,1)} %q_ref.3) | copy-start | bytes 1572868
  2.6 21.6 %copy-start.2 = (s32[4]{0:T(128)S(1)}, s32[4]{0:T(128)}, u32[]{:S(2)}) copy-start(s32[4]{0:T(128)} %doc_ref.3) | copy-start | bytes 52
  2.7 21.6 %copy-start.3 = (s32[1,35]{1,0:T(1,128)S(1)}, s32[1,35]{1,0:T(1,128)}, u32[]{:S(2)}) copy-start(s32[1,35]{1,0:T(1,128)} %list_ref.3) | copy-start | bytes 424
  2.7 13.2 %collective-permute-start.1 = (bf16[1024,128]{1,0:T(8,128)(2,1)S(1)}, bf16[1024,128]{1,0:T(8,128)(2,1)S(1)}, u32[]{:S(2)}, u32[]{:S(2)}) collective-permute-start(bf16[1024,128]{1,0:T(8,128)(2,1)S(1)} %pad_maximum_fusion.1.own), channel_id=1, source_target_pairs={{0,32},{1,65},{2,34},{3,67},{4,36},{5,69},{6,38},{7,71},{8,40},{9,... | collective-permute-start | bytes 786440 | tf_op jit(solution)/shard_map/ppermute | solution.py:36
  15.9 1.9 %collective-permute-start.2 = (bf16[1024,128]{1,0:T(8,128)(2,1)S(1)}, bf16[1024,128]{1,0:T(8,128)(2,1)S(1)}, u32[]{:S(2)}, u32[]{:S(2)}) collective-permute-start(bf16[1024,128]{1,0:T(8,128)(2,1)S(1)} %collective-permute-done.1.mine), channel_id=1, source_target_pairs={{0,1},{1,0},{2,3},{3,2},{4,5},{5,4},{6,7},{7,6},{8,9},{9,8},{10,11... | collective-permute-start | bytes 786440 | tf_op jit(solution)/shard_map/ppermute | solution.py:36
  15.9 8.4 %collective-permute-start = (bf16[512,512]{1,0:T(8,128)(2,1)}, bf16[512,512]{1,0:T(8,128)(2,1)}, u32[]{:S(2)}, u32[]{:S(2)}) collective-permute-start(bf16[512,512]{1,0:T(8,128)(2,1)} %q_ref.3), channel_id=1, source_target_pairs={{0,1},{1,0},{2,3},{3,2},{4,5},{5,4},{6,7},{7,6},{8,9},{9,8},{10,11... | collective-permute-start | bytes 1572872 | tf_op jit(solution)/shard_map/ppermute | solution.py:36
  16.4 37.3 %collective-permute-start.8 = (bf16[512,2048]{1,0:T(8,128)(2,1)S(1)}, bf16[512,2048]{1,0:T(8,128)(2,1)}, u32[]{:S(2)}, u32[]{:S(2)}) collective-permute-start(bf16[512,2048]{1,0:T(8,128)(2,1)S(1)} %copy-done), channel_id=1, source_target_pairs={{0,1},{1,0},{2,3},{3,2},{4,5},{5,4},{6,7},{7,6},{8,9},{9,8},{10,11... | collective-permute-start | bytes 6291464 | tf_op jit(solution)/shard_map/ppermute | solution.py:36
  19.9 17.1 %collective-permute-start.3 = (bf16[2048,128]{1,0:T(8,128)(2,1)S(1)}, bf16[2048,128]{1,0:T(8,128)(2,1)S(1)}, u32[]{:S(2)}, u32[]{:S(2)}) collective-permute-start(bf16[2048,128]{1,0:T(8,128)(2,1)S(1)} %pad_maximum_fusion), channel_id=1, source_target_pairs={{0,8},{1,25},{2,10},{3,27},{4,12},{5,29},{6,14},{7,31},{8,16},{9,1... | collective-permute-start | bytes 1572872 | tf_op jit(solution)/shard_map/ppermute | solution.py:36
  21.5 15.5 %collective-permute-start.4 = (bf16[1024,128]{1,0:T(8,128)(2,1)S(1)}, bf16[1024,128]{1,0:T(8,128)(2,1)S(1)}, u32[]{:S(2)}, u32[]{:S(2)}) collective-permute-start(bf16[1024,128]{1,0:T(8,128)(2,1)S(1)} %get-tuple-element.23), channel_id=1, source_target_pairs={{0,16},{1,17},{2,18},{3,19},{4,20},{5,21},{6,22},{7,23},{8,24},{9,... | collective-permute-start | bytes 786440 | tf_op jit(solution)/shard_map/ppermute | solution.py:36
  37.0 2.3 %collective-permute-start.5 = (bf16[2048,128]{1,0:T(8,128)(2,1)S(1)}, bf16[2048,128]{1,0:T(8,128)(2,1)S(1)}, u32[]{:S(2)}, u32[]{:S(2)}) collective-permute-start(bf16[2048,128]{1,0:T(8,128)(2,1)S(1)} %collective-permute-done.3.rest_0_), channel_id=1, source_target_pairs={{0,1},{1,0},{2,3},{3,2},{4,5},{5,4},{6,7},{7,6},{8,9},{9,8},{10,11... | collective-permute-start | bytes 1572872 | tf_op jit(solution)/shard_map/ppermute | solution.py:36
  37.0 2.3 %collective-permute-start.6 = (bf16[1024,128]{1,0:T(8,128)(2,1)S(1)}, bf16[1024,128]{1,0:T(8,128)(2,1)S(1)}, u32[]{:S(2)}, u32[]{:S(2)}) collective-permute-start(bf16[1024,128]{1,0:T(8,128)(2,1)S(1)} %collective-permute-done.4.rest_1_), channel_id=1, source_target_pairs={{0,1},{1,0},{2,3},{3,2},{4,5},{5,4},{6,7},{7,6},{8,9},{9,8},{10,11... | collective-permute-start | bytes 786440 | tf_op jit(solution)/shard_map/ppermute | solution.py:36
  51.7 2.0 %collective-permute-start.7 = (bf16[256,1024]{1,0:T(8,128)(2,1)S(1)}, bf16[256,1024]{1,0:T(8,128)(2,1)S(1)}, u32[]{:S(2)}, u32[]{:S(2)}) collective-permute-start(bf16[256,1024]{1,0:T(8,128)(2,1)S(1)} %far.1.ho_ref), channel_id=1, source_target_pairs={{0,1},{1,0},{2,3},{3,2},{4,5},{5,4},{6,7},{7,6},{8,9},{9,8},{10,11... | collective-permute-start | bytes 1572872 | tf_op jit(solution)/shard_map/ppermute | solution.py:36
  57.6 12.8 %collective-permute-start.9 = (bf16[512,256]{1,0:T(8,128)(2,1)S(1)}, bf16[512,256]{1,0:T(8,128)(2,1)S(1)}, u32[]{:S(2)}, u32[]{:S(2)}) collective-permute-start(bf16[512,256]{1,0:T(8,128)(2,1)S(1)} %get-tuple-element.21), channel_id=1, source_target_pairs={{0,2},{1,7},{2,4},{3,1},{4,6},{5,3},{6,0},{7,5},{8,10},{9,15},{10,... | collective-permute-start | bytes 786440 | tf_op jit(solution)/shard_map/ppermute | solution.py:36
  60.9 12.3 %collective-permute-start.11 = (bf16[512,256]{1,0:T(8,128)(2,1)S(1)}, bf16[512,256]{1,0:T(8,128)(2,1)S(1)}, u32[]{:S(2)}, u32[]{:S(2)}) collective-permute-start(bf16[512,256]{1,0:T(8,128)(2,1)S(1)} %get-tuple-element.22), channel_id=1, source_target_pairs={{0,2},{1,7},{2,4},{3,1},{4,6},{5,3},{6,0},{7,5},{8,10},{9,15},{10,... | collective-permute-start | bytes 786440 | tf_op jit(solution)/shard_map/ppermute | solution.py:36
  70.5 10.6 %collective-permute-start.10 = (bf16[512,256]{1,0:T(8,128)(2,1)S(1)}, bf16[512,256]{1,0:T(8,128)(2,1)S(1)}, u32[]{:S(2)}, u32[]{:S(2)}) collective-permute-start(bf16[512,256]{1,0:T(8,128)(2,1)S(1)} %add_convert_fusion.1), channel_id=1, source_target_pairs={{0,2},{1,7},{2,4},{3,1},{4,6},{5,3},{6,0},{7,5},{8,10},{9,15},{10,... | collective-permute-start | bytes 786440 | tf_op jit(solution)/shard_map/ppermute | solution.py:36
  73.3 7.9 %collective-permute-start.12 = (bf16[512,256]{1,0:T(8,128)(2,1)S(1)}, bf16[512,256]{1,0:T(8,128)(2,1)S(1)}, u32[]{:S(2)}, u32[]{:S(2)}) collective-permute-start(bf16[512,256]{1,0:T(8,128)(2,1)S(1)} %collective-permute-done.11), channel_id=1, source_target_pairs={{0,1},{1,0},{2,3},{3,2},{4,5},{5,4},{6,7},{7,6},{8,9},{9,8},{10,11... | collective-permute-start | bytes 786440 | tf_op jit(solution)/shard_map/ppermute | solution.py:36

commit v3 on v2

--- a/solution.py
+++ b/solution.py
@@ -19,6 +19,7 @@
 EXP_SCALE = math.log2(math.e) / math.sqrt(HEAD_WIDTH)
 AXES = ("ctx", "head")
 X_CHIPS = 4
+TURNS = (1, 3, 2)
 GRANT = 40 * 2**20
 
 
@@ -36,24 +37,15 @@
     return lax.ppermute(block, AXES, ctx_head_pairs(n_ctx, n_head, route))
 
 
-def to_later_rows(n_ctx):
+def rows_on(n_ctx, shards):
+    return lambda c, h: (c + shards, h) if c + shards < n_ctx else None
+
+
+def turned(by):
     def route(c, h):
-        d = c + 4 + 4 * (h % 2)
-        return (d, h) if d < n_ctx else None
+        return (c - c % X_CHIPS + (c + by) % X_CHIPS, h)
 
     return route
-
-
-def turned(c, by):
-    return c - c % X_CHIPS + (c + by) % X_CHIPS
-
-
-def beside(c, h):
-    return (turned(c, 1 if h % 2 == 0 else 3), h)
-
-
-def across(c, h):
-    return (turned(c, 2), h)
 
 
 def other_core(c, h):
@@ -112,12 +104,14 @@
         )
 
 
-def load_shard(copies, ref, first, kx, vx, row):
-    copies.start(ref.at[pl.ds(first, SHARD)], kx.at[pl.ds(row, SHARD)])
-    copies.start(
-        ref.at[pl.ds(first + SHARD, SHARD)],
-        vx.at[pl.ds(row, SHARD), pl.ds(0, HEAD_WIDTH)],
-    )
+def load_shard(copies, mine, theirs, first, kx, vx, row, core):
+    for ref, which in ((mine, core), (theirs, 1 - core)):
+        at = pl.multiple_of(row + which * HALF, HALF)
+        copies.start(ref.at[pl.ds(first, HALF)], kx.at[pl.ds(at, HALF)])
+        copies.start(
+            ref.at[pl.ds(first + HALF, HALF)],
+            vx.at[pl.ds(at, HALF), pl.ds(0, HEAD_WIDTH)],
+        )
 
 
 def softmax_tile(q, k, v, mask, m, acc):
@@ -135,24 +129,23 @@
     return slice(g * HEAD_WIDTH, (g + 1) * HEAD_WIDTH)
 
 
-def turn_distances(core):
-    return [jnp.where(core == 0, a, b) for a, b in ((1, 3), (5, 7), (2, 6))]
-
-
 def load_queries(copies, q_ref, rq_ref, row, rows, qs):
     at = pl.multiple_of(row, BLK)
     copies.start(q_ref.at[pl.ds(at, rows)], qs.at[:, pl.ds(0, 512)])
     copies.start(rq_ref.at[pl.ds(at, rows)], qs.at[:, pl.ds(512, 512)])
 
 
-def near_kernel(doc_ref, list_ref, q_ref, rq_ref, own, mine, theirs, *rest):
+def near_kernel(doc_ref, list_ref, q_ref, rq_ref, k_ref, v_ref, *rest):
+    four, eight, their_four, their_eight = rest[:4]
+    rest = rest[4:]
     acc_ref, ml_ref, kx, vx, qs, mask, sem = rest
     ctx, z, core = position()
     copies = Copies(sem)
     load_queries(copies, q_ref, rq_ref, core * HALF, HALF, qs)
-    load_shard(copies, own, 0, kx, vx, 0)
-    load_shard(copies, mine, 0, kx, vx, pl.multiple_of((1 + core) * SHARD, SHARD))
-    load_shard(copies, theirs, 0, kx, vx, pl.multiple_of((2 - core) * SHARD, SHARD))
+    copies.start(k_ref, kx.at[pl.ds(0, SHARD)])
+    copies.start(v_ref, vx.at[pl.ds(0, SHARD), pl.ds(0, HEAD_WIDTH)])
+    load_shard(copies, four, their_four, 0, kx, vx, SHARD, core)
+    load_shard(copies, eight, their_eight, 0, kx, vx, 2 * SHARD, core)
     vx[:, HEAD_WIDTH:] = jnp.ones((vx.shape[0], HEAD_WIDTH), jnp.bfloat16)
     lane = lax.broadcasted_iota(jnp.int32, (BLK, HEAD_WIDTH), 1)
     list_last = last_listed(list_ref)
@@ -194,20 +187,20 @@
 
 
 def far_kernel(doc_ref, list_ref, q_ref, rq_ref, *rest):
-    turns, (acc_in, ml_in, ho) = rest[:4], rest[4:7]
-    kx, vx, qs, bias, acc_s, ml_s, sem = rest[7:]
+    mine, theirs, (acc_in, ml_in, ho) = rest[:3], rest[3:6], rest[6:9]
+    kx, vx, qs, bias, acc_s, ml_s, sem = rest[9:]
     ctx, z, core = position()
     copies = Copies(sem)
-    for i in range(2):
-        at = 3 * i * SHARD
-        load_shard(copies, turns[2 * i], 0, kx, vx, at)
-        load_shard(copies, turns[2 * i], 2 * SHARD, kx, vx, at + SHARD)
-        load_shard(copies, turns[2 * i + 1], 0, kx, vx, at + 2 * SHARD)
+    distances = []
+    for by, a, b in zip(TURNS, mine, theirs):
+        for part in range(2):
+            at = len(distances) * SHARD
+            load_shard(copies, a, b, part * SHARD, kx, vx, at, core)
+            distances.append(by + 4 * part)
     load_queries(copies, q_ref, rq_ref, core * HALF, HALF, qs)
     copies.start(acc_in, acc_s)
     copies.start(ml_in, ml_s)
     vx[:, HEAD_WIDTH:] = jnp.ones((vx.shape[0], HEAD_WIDTH), jnp.bfloat16)
-    distances = turn_distances(core) + turn_distances(1 - core)
     list_last = last_listed(list_ref)
     for ii in range(2):
         lo, hi = block_range(doc_ref, list_ref, list_last, ctx, core * 2 + ii)
@@ -290,7 +283,7 @@
     scratch = key_scratch(3 * SHARD) + [
         pltpu.VMEM((HALF, 1024), jnp.bfloat16),
         pltpu.VMEM((BLK, 3 * SHARD), jnp.float32),
-        pltpu.SemaphoreType.DMA((8,)),
+        pltpu.SemaphoreType.DMA((12,)),
     ]
     return call(near_kernel, "near", STATE, scratch, 3 * SHARD, HALF, args)
 
@@ -301,7 +294,7 @@
         pltpu.VMEM((2, 8, 6 * SHARD), jnp.float32),
         pltpu.VMEM((HALF, 1024), jnp.float32),
         pltpu.VMEM((HALF, HEAD_WIDTH), jnp.float32),
-        pltpu.SemaphoreType.DMA((16,)),
+        pltpu.SemaphoreType.DMA((28,)),
     ]
     out = jax.ShapeDtypeStruct((HALF, 1024), jnp.bfloat16)
     return call(far_kernel, "far", [out], scratch, 6 * SHARD, HALF, args)[0]
@@ -340,36 +333,33 @@
     def go(block, route):
         return send(block, n_ctx, n_head, route)
 
-    def pick(first, *arrays):
-        return [jnp.where(first, a, b) for a, b in zip(arrays[:-1], arrays[1:])]
-
+    own_k, own_v = (
+        lax.dynamic_index_in_dim(a, z, 1, keepdims=False)
+        for a in (key_rows, value_vectors)
+    )
     own = jnp.concatenate(
-        [
-            lax.dynamic_index_in_dim(a, z, 1, keepdims=False)
-            for a in (key_rows, value_vectors)
-        ]
+        [lax.dynamic_slice_in_dim(a, core * HALF, HALF, 0) for a in (own_k, own_v)]
     )
     rq = go(queries, other_core)
     rw = go(out_weight, other_core)
-    row_mine = go(own, to_later_rows(n_ctx))
-    row_theirs = go(row_mine, other_core)
-    four = jnp.where(core == 0, row_mine, row_theirs)
-    eight = jnp.where(core == 0, row_theirs, row_mine)
-    wraps = jnp.where(core == 0, x == X_CHIPS - 1, x >= 1)
-    beside_load = jnp.concatenate(
-        [jnp.where(wraps, four, own), jnp.where(wraps, eight, four)]
-    )
-    wraps = x >= X_CHIPS // 2
-    across_load = jnp.where(
-        core == 0, jnp.where(wraps, four, own), jnp.where(wraps, eight, four)
-    )
-    near_turn = go(beside_load, beside)
-    far_turn = go(across_load, across)
-    acc, ml = near(doc_start, block_list, queries, rq, own, row_mine, row_theirs)
-    near_turn, far_turn, acc = lax.optimization_barrier((near_turn, far_turn, acc))
-    turns = (
-        near_turn, far_turn, go(near_turn, other_core), go(far_turn, other_core)
-    )
+    four = go(own, rows_on(n_ctx, 4))
+    eight = go(own, rows_on(n_ctx, 8))
+    loads = []
+    for by in TURNS:
+        wraps = x + by >= X_CHIPS
+        loads.append(
+            jnp.concatenate(
+                [jnp.where(wraps, four, own), jnp.where(wraps, eight, four)]
+            )
+        )
+    *loads, own_k = lax.optimization_barrier((*loads, own_k))
+    turns = [go(load, turned(by)) for load, by in zip(loads, TURNS)]
+    acc, ml = near(
+        doc_start, block_list, queries, rq, own_k, own_v,
+        four, eight, go(four, other_core), go(eight, other_core),
+    )
+    *turns, acc = lax.optimization_barrier((*turns, acc))
+    turns += [go(t, other_core) for t in turns]
     ho = far(doc_start, block_list, queries, rq, *turns, acc, ml)
     relay, plain, fwd, keep = project(ho, go(ho, other_core), out_weight, rw)
     came = go(relay, along_z(n_head))

time: 82.1 us -> 77 us (0.938)
  waiting for transfers between devices: 35.3 us -> 27.1 us
  starting transfers between devices: 17.9 us -> 23.1 us
  other arithmetic: 3.06 us -> 1.74 us
  Pallas kernels: 22.9 us -> 21.7 us
    ppermute x13 -> x17, waiting for transfers between devices: 35.3 us -> 27.1 us  [send(): return lax.ppermute(block, AXES, ctx_head_pairs(n_ctx, n_head, route))]
    ppermute x13 -> x17, starting transfers between devices: 17.9 us -> 23.1 us  [send(): return lax.ppermute(block, AXES, ctx_head_pairs(n_ctx, n_head, route))]
    dynamic_slice x0 -> x1, local copies, waits for them, and re-layouts: none -> 1.3 us  [on_device(): lax.dynamic_slice_in_dim(a, core * HALF, HALF, 0)]
    select_n x1 -> x0, other arithmetic: 1.08 us -> none  [on_device(): jnp.where(core == 0, jnp.where(wraps, four, own), jnp.where(wraps, eight,...]
    select_n x1, other arithmetic: 1.07 us -> 0.13 us  [on_device(): jnp.where(wraps, four, own)]
    dynamic_slice x1 -> x2, local copies, waits for them, and re-layouts: 1.89 us -> 1.59 us  [on_device(): lax.dynamic_index_in_dim(a, z, 1, keepdims=False)]
  transfers between devices with their start and end apart: 13 -> 17, of which waited for: 8 -> 11; matrix products, arithmetic and copies ran while one was open for 3% -> 2% of each run, Pallas kernels for 23% -> 24%
where the time goes in v3:
time: 77 us; the launch traced here: 76.8 us
  waiting for transfers between devices  27.1 us (35%)
  starting transfers between devices  23.1 us (30%)
  Pallas kernels  21.7 us (28%)
  local copies, waits for them, and re-layouts  2.98 us (4%)
  other arithmetic  1.74 us (2%)
    ppermute x17, waiting for transfers between devices, send(): return lax.ppermute(block, AXES, ctx_head_pairs(n_ctx, n_head, route))  27.1 us
    ppermute x17, starting transfers between devices, send(): return lax.ppermute(block, AXES, ctx_head_pairs(n_ctx, n_head, route))  23.1 us
    pallas_call x2, Pallas kernels, call(): pl.pallas_call(kernel, out_shape=out_shape, in_specs=[SMEM, SMEM] + [ANY]...  18.4 us
    pallas_call x1, Pallas kernels, project(): pl.pallas_call(project_kernel, out_shape=[out] * 4, in_specs=[ANY] * 4, o...  3.26 us
    dynamic_slice x2, local copies, waits for them, and re-layouts, on_device(): lax.dynamic_index_in_dim(a, z, 1, keepdims=False)  1.59 us
  transfers between devices with their start and end apart: 17, of which 11 were waited for; matrix products, arithmetic and copies ran while one was open for 2% of the time, Pallas kernels for 24%

profile of v3, /device:TPU:32, one launch (start us, length us, event | category | flops | bytes accessed | tf_op | source)
XLA Modules:
  0.0 76.8 jit_solution(4481268324036683695)
XLA Ops:
  0.0 1.3 %constant_dynamic-slice_fusion.2 = (bf16[256,1,128]{2,1,0:T(2,128)(2,1)S(1)}, bf16[256,1,128]{2,1,0:T(2,128)(2,1)S(1)}) fusion(bf16[512,4,128]{2,1,0:T(4,128)(2,1)} %param.8, s32[]{:T(128)S(6)} %select_n.64, s32[]{:T(128)S(6)} %select_n.67, bf16[512,4,128]{2,1,0:T(4,128)(2,1)} %param.7), kind=kLoop, calls=%fused_computation.18 | loop fusion | bytes 262152 | tf_op jit(solution)/shard_map/dynamic_slice | solution.py:341
  1.3 0.0 copy-start.4
  1.4 0.7 pad_maximum_fusion.3
  2.0 5.1 %collective-permute-start.2 = (bf16[512,128]{1,0:T(8,128)(2,1)}, bf16[512,128]{1,0:T(8,128)(2,1)S(1)}, u32[]{:S(2)}, u32[]{:S(2)}) collective-permute-start(bf16[512,128]{1,0:T(8,128)(2,1)} %pad_maximum_fusion.3), channel_id=1, source_target_pairs={{0,64},{1,65},{2,66},{3,67},{4,68},{5,69},{6,70},{7,71},{8,72},{9,... | collective-permute-start | bytes 393224 | tf_op jit(solution)/shard_map/ppermute | solution.py:37
  7.1 2.6 %collective-permute-start.1 = (bf16[512,128]{1,0:T(8,128)(2,1)}, bf16[512,128]{1,0:T(8,128)(2,1)S(1)}, u32[]{:S(2)}, u32[]{:S(2)}) collective-permute-start(bf16[512,128]{1,0:T(8,128)(2,1)} %pad_maximum_fusion.3), channel_id=1, source_target_pairs={{0,32},{1,33},{2,34},{3,35},{4,36},{5,37},{6,38},{7,39},{8,40},{9,... | collective-permute-start | bytes 393224 | tf_op jit(solution)/shard_map/ppermute | solution.py:37
  9.7 0.1 collective-permute-start.12
  9.8 0.5 collective-permute-start
  10.3 1.3 %constant_dynamic-slice_fusion.1 = bf16[512,1,128]{2,1,0:T(2,128)(2,1)S(1)} fusion(bf16[512,4,128]{2,1,0:T(4,128)(2,1)} %param.7, s32[]{:T(128)S(6)} %select_n.66), kind=kLoop, calls=%fused_computation.17 | loop fusion | bytes 262148 | tf_op jit(solution)/shard_map/jit(dynamic_index_in_dim)/dynamic_slice | solution.py:337
  11.6 0.0 copy-start.1
  11.6 0.0 copy-start.2
  11.7 0.0 copy-start.3
  11.7 0.2 collective-permute-done.2.rest_1_
  11.9 0.0 collective-permute-start.7
  11.9 4.4 %collective-permute-done.1.rest_0_ = bf16[512,128]{1,0:T(8,128)(2,1)S(1)} collective-permute-done((bf16[512,128]{1,0:T(8,128)(2,1)}, bf16[512,128]{1,0:T(8,128)(2,1)S(1)}, u32[]{:S(2)}, u32[]{:S(2)}) %collective-permute-start.1) | collective-permute-done | bytes 131104 | tf_op jit(solution)/shard_map/ppermute | solution.py:37
  16.3 0.0 collective-permute-start.6
  16.3 0.1 broadcast_select_fusion.1
  16.5 1.6 %collective-permute-start.3 = (bf16[1024,128]{1,0:T(8,128)(2,1)S(1)}, bf16[1024,128]{1,0:T(8,128)(2,1)S(1)}, u32[]{:S(2)}, u32[]{:S(2)}) collective-permute-start(bf16[1024,128]{1,0:T(8,128)(2,1)S(1)} %pad_maximum_fusion), channel_id=1, source_target_pairs={{0,8},{1,9},{2,10},{3,11},{4,12},{5,13},{6,14},{7,15},{8,16},{9,17... | collective-permute-start | bytes 786440 | tf_op jit(solution)/shard_map/ppermute | solution.py:37
  18.1 0.0 collective-permute-done.7.rest_3_
  18.1 1.7 %collective-permute-start.4 = (bf16[1024,128]{1,0:T(8,128)(2,1)S(1)}, bf16[1024,128]{1,0:T(8,128)(2,1)S(1)}, u32[]{:S(2)}, u32[]{:S(2)}) collective-permute-start(bf16[1024,128]{1,0:T(8,128)(2,1)S(1)} %pad_maximum_fusion.1), channel_id=1, source_target_pairs={{0,24},{1,25},{2,26},{3,27},{4,28},{5,29},{6,30},{7,31},{8,0},{9,1... | collective-permute-start | bytes 786440 | tf_op jit(solution)/shard_map/ppermute | solution.py:37
  19.8 0.0 collective-permute-done.6.rest_2_
  19.8 1.8 %collective-permute-start.5 = (bf16[1024,128]{1,0:T(8,128)(2,1)S(1)}, bf16[1024,128]{1,0:T(8,128)(2,1)S(1)}, u32[]{:S(2)}, u32[]{:S(2)}) collective-permute-start(bf16[1024,128]{1,0:T(8,128)(2,1)S(1)} %pad_maximum_fusion.2), channel_id=1, source_target_pairs={{0,16},{1,17},{2,18},{3,19},{4,20},{5,21},{6,22},{7,23},{8,24},{9,... | collective-permute-start | bytes 786440 | tf_op jit(solution)/shard_map/ppermute | solution.py:37
  21.7 0.3 constant_dynamic-slice_fusion
  22.0 0.0 collective-permute-done.rq_ref
  22.0 6.5 %near.1 = (f32[256,1024]{1,0:T(8,128)S(1)}, f32[256,128]{1,0:T(8,128)S(1)}) custom-call(s32[4]{0:T(128)S(1)} %copy-done.2, s32[1,35]{1,0:T(1,128)S(1)} %copy-done.3, bf16[512,512]{1,0:T(8,128)(2,1)S(1)} %copy-done.1, bf16[512,512]{1,0:T(8,128)(2,1)S(1)} %collective-permute-done.rq_ref, bf16[512,128]{1,0:T(8,128)(2,1)S(1)} %bitcast.12, ...), custom_call_target="tpu_custom_call" | custom-call | flops 1610612736 | bytes 4194304 | tf_op jit(solution)/shard_map/near/pallas_call | solution.py:266
  28.5 0.0 collective-permute-done.3.rest_0_
  28.5 2.9 %collective-permute-done.4.rest_1_ = bf16[1024,128]{1,0:T(8,128)(2,1)S(1)} collective-permute-done((bf16[1024,128]{1,0:T(8,128)(2,1)S(1)}, bf16[1024,128]{1,0:T(8,128)(2,1)S(1)}, u32[]{:S(2)}, u32[]{:S(2)}) %collective-permute-start.4) | collective-permute-done | bytes 262176 | tf_op jit(solution)/shard_map/ppermute | solution.py:37
  31.4 1.7 %collective-permute-done.5.rest_2_ = bf16[1024,128]{1,0:T(8,128)(2,1)S(1)} collective-permute-done((bf16[1024,128]{1,0:T(8,128)(2,1)S(1)}, bf16[1024,128]{1,0:T(8,128)(2,1)S(1)}, u32[]{:S(2)}, u32[]{:S(2)}) %collective-permute-start.5) | collective-permute-done | bytes 262176 | tf_op jit(solution)/shard_map/ppermute | solution.py:37
  33.1 0.0 collective-permute-start.8
  33.1 0.5 collective-permute-start.9
  33.6 0.0 collective-permute-start.10
  33.6 1.0 %collective-permute-done.8.rest_3_ = bf16[1024,128]{1,0:T(8,128)(2,1)S(1)} collective-permute-done((bf16[1024,128]{1,0:T(8,128)(2,1)S(1)}, bf16[1024,128]{1,0:T(8,128)(2,1)S(1)}, u32[]{:S(2)}, u32[]{:S(2)}) %collective-permute-start.8) | collective-permute-done | bytes 262176 | tf_op jit(solution)/shard_map/ppermute | solution.py:37
  34.7 0.4 collective-permute-done.9.rest_4_
  35.0 0.4 collective-permute-done.10.rest_5_
  35.4 11.9 %far.1.ho_ref = bf16[256,1024]{1,0:T(8,128)(2,1)S(1)} custom-call(s32[4]{0:T(128)S(1)} %copy-done.2, s32[1,35]{1,0:T(1,128)S(1)} %copy-done.3, bf16[512,512]{1,0:T(8,128)(2,1)S(1)} %copy-done.1, bf16[512,512]{1,0:T(8,128)(2,1)S(1)} %collective-permute-done.rq_ref, bf16[1024,128]{1,0:T(8,128)(2,1)S(1)} %collective-permute-done.3.rest_0_, ...), custom_call_target="tpu_custom_call" | custom-call | flops 3221225472 | bytes 4194304 | tf_op jit(solution)/shard_map/far/pallas_call | solution.py:266
  47.4 0.2 collective-permute-start.11
  47.6 1.8 %collective-permute-done.11.got_ref = bf16[256,1024]{1,0:T(8,128)(2,1)S(1)} collective-permute-done((bf16[256,1024]{1,0:T(8,128)(2,1)S(1)}, bf16[256,1024]{1,0:T(8,128)(2,1)S(1)}, u32[]{:S(2)}, u32[]{:S(2)}) %collective-permute-start.11) | collective-permute-done | bytes 524320 | tf_op jit(solution)/shard_map/ppermute | solution.py:37
  49.4 0.0 collective-permute-done.12.rw_ref
  49.4 3.3 %project.1 = (bf16[512,256]{1,0:T(8,128)(2,1)S(1)}, bf16[512,256]{1,0:T(8,128)(2,1)S(1)}, bf16[512,256]{1,0:T(8,128)(2,1)S(1)}, bf16[512,256]{1,0:T(8,128)(2,1)S(1)}) custom-call(bf16[256,1024]{1,0:T(8,128)(2,1)S(1)} %far.1.ho_ref, bf16[256,1024]{1,0:T(8,128)(2,1)S(1)} %collective-permute-done.11.got_ref, bf16[512,2048]{1,0:T(8,128)(2,1)S(1)} %copy-done, ...), custom_call_target="tpu_custom_call" | custom-call | flops 1000000000 | bytes 4194304 | tf_op jit(solution)/shard_map/project/pallas_call | solution.py:305
  52.6 3.3 %collective-permute-start.13 = (bf16[512,256]{1,0:T(8,128)(2,1)S(1)}, bf16[512,256]{1,0:T(8,128)(2,1)S(1)}, u32[]{:S(2)}, u32[]{:S(2)}) collective-permute-start(bf16[512,256]{1,0:T(8,128)(2,1)S(1)} %get-tuple-element.31), channel_id=1, source_target_pairs={{0,2},{1,7},{2,4},{3,1},{4,6},{5,3},{6,0},{7,5},{8,10},{9,15},{10,... | collective-permute-start | bytes 786440 | tf_op jit(solution)/shard_map/ppermute | solution.py:37
  56.0 3.6 %collective-permute-start.15 = (bf16[512,256]{1,0:T(8,128)(2,1)S(1)}, bf16[512,256]{1,0:T(8,128)(2,1)S(1)}, u32[]{:S(2)}, u32[]{:S(2)}) collective-permute-start(bf16[512,256]{1,0:T(8,128)(2,1)S(1)} %get-tuple-element.32), channel_id=1, source_target_pairs={{0,2},{1,7},{2,4},{3,1},{4,6},{5,3},{6,0},{7,5},{8,10},{9,15},{10,... | collective-permute-start | bytes 786440 | tf_op jit(solution)/shard_map/ppermute | solution.py:37
  59.6 5.7 %collective-permute-done.13 = bf16[512,256]{1,0:T(8,128)(2,1)S(1)} collective-permute-done((bf16[512,256]{1,0:T(8,128)(2,1)S(1)}, bf16[512,256]{1,0:T(8,128)(2,1)S(1)}, u32[]{:S(2)}, u32[]{:S(2)}) %collective-permute-start.13) | collective-permute-done | bytes 262176 | tf_op jit(solution)/shard_map/ppermute | solution.py:37
  65.3 0.1 add_convert_fusion.1
  65.4 0.9 %collective-permute-start.14 = (bf16[512,256]{1,0:T(8,128)(2,1)S(1)}, bf16[512,256]{1,0:T(8,128)(2,1)S(1)}, u32[]{:S(2)}, u32[]{:S(2)}) collective-permute-start(bf16[512,256]{1,0:T(8,128)(2,1)S(1)} %add_convert_fusion.1), channel_id=1, source_target_pairs={{0,2},{1,7},{2,4},{3,1},{4,6},{5,3},{6,0},{7,5},{8,10},{9,15},{10,... | collective-permute-start | bytes 786440 | tf_op jit(solution)/shard_map/ppermute | solution.py:37
  66.3 1.8 %collective-permute-done.15 = bf16[512,256]{1,0:T(8,128)(2,1)S(1)} collective-permute-done((bf16[512,256]{1,0:T(8,128)(2,1)S(1)}, bf16[512,256]{1,0:T(8,128)(2,1)S(1)}, u32[]{:S(2)}, u32[]{:S(2)}) %collective-permute-start.15) | collective-permute-done | bytes 262176 | tf_op jit(solution)/shard_map/ppermute | solution.py:37
  68.1 1.0 %collective-permute-start.16 = (bf16[512,256]{1,0:T(8,128)(2,1)S(1)}, bf16[512,256]{1,0:T(8,128)(2,1)S(1)}, u32[]{:S(2)}, u32[]{:S(2)}) collective-permute-start(bf16[512,256]{1,0:T(8,128)(2,1)S(1)} %collective-permute-done.15), channel_id=1, source_target_pairs={{0,1},{1,0},{2,3},{3,2},{4,5},{5,4},{6,7},{7,6},{8,9},{9,8},{10,11... | collective-permute-start | bytes 786440 | tf_op jit(solution)/shard_map/ppermute | solution.py:37
  69.2 6.8 %collective-permute-done.14 = bf16[512,256]{1,0:T(8,128)(2,1)S(1)} collective-permute-done((bf16[512,256]{1,0:T(8,128)(2,1)S(1)}, bf16[512,256]{1,0:T(8,128)(2,1)S(1)}, u32[]{:S(2)}, u32[]{:S(2)}) %collective-permute-start.14) | collective-permute-done | bytes 262176 | tf_op jit(solution)/shard_map/ppermute | solution.py:37
  76.0 0.0 collective-permute-done.16
  76.0 0.8 %add_convert_fusion = bf16[512,256]{1,0:T(8,128)(2,1)} fusion(bf16[512,256]{1,0:T(8,128)(2,1)S(1)} %collective-permute-done.16, bf16[512,256]{1,0:T(8,128)(2,1)S(1)} %collective-permute-done.14, bf16[512,256]{1,0:T(8,128)(2,1)S(1)} %get-tuple-element.29), kind=kLoop, calls=%fused_computation | loop fusion | flops 786432 | bytes 1048576 | tf_op jit(solution)/shard_map/convert_element_type | solution.py:324
  (13 shorter events, 0.1 us)
Async XLA Ops:
  1.3 20.3 %copy-start.4 = (bf16[512,4,128]{2,1,0:T(4,128)(2,1)S(1)}, bf16[512,4,128]{2,1,0:T(4,128)(2,1)}, u32[]{:S(2)}) copy-start(bf16[512,4,128]{2,1,0:T(4,128)(2,1)} %param.8) | copy-start | bytes 1572868
  2.0 9.8 %collective-permute-start.2 = (bf16[512,128]{1,0:T(8,128)(2,1)}, bf16[512,128]{1,0:T(8,128)(2,1)S(1)}, u32[]{:S(2)}, u32[]{:S(2)}) collective-permute-start(bf16[512,128]{1,0:T(8,128)(2,1)} %pad_maximum_fusion.3), channel_id=1, source_target_pairs={{0,64},{1,65},{2,66},{3,67},{4,68},{5,69},{6,70},{7,71},{8,72},{9,... | collective-permute-start | bytes 393224 | tf_op jit(solution)/shard_map/ppermute | solution.py:37
  7.1 9.2 %collective-permute-start.1 = (bf16[512,128]{1,0:T(8,128)(2,1)}, bf16[512,128]{1,0:T(8,128)(2,1)S(1)}, u32[]{:S(2)}, u32[]{:S(2)}) collective-permute-start(bf16[512,128]{1,0:T(8,128)(2,1)} %pad_maximum_fusion.3), channel_id=1, source_target_pairs={{0,32},{1,33},{2,34},{3,35},{4,36},{5,37},{6,38},{7,39},{8,40},{9,... | collective-permute-start | bytes 393224 | tf_op jit(solution)/shard_map/ppermute | solution.py:37
  9.7 39.7 %collective-permute-start.12 = (bf16[512,2048]{1,0:T(8,128)(2,1)}, bf16[512,2048]{1,0:T(8,128)(2,1)S(1)}, u32[]{:S(2)}, u32[]{:S(2)}) collective-permute-start(bf16[512,2048]{1,0:T(8,128)(2,1)} %w_ref.1), channel_id=1, source_target_pairs={{0,1},{1,0},{2,3},{3,2},{4,5},{5,4},{6,7},{7,6},{8,9},{9,8},{10,11... | collective-permute-start | bytes 6291464 | tf_op jit(solution)/shard_map/ppermute | solution.py:37
  9.8 12.2 %collective-permute-start = (bf16[512,512]{1,0:T(8,128)(2,1)}, bf16[512,512]{1,0:T(8,128)(2,1)S(1)}, u32[]{:S(2)}, u32[]{:S(2)}) collective-permute-start(bf16[512,512]{1,0:T(8,128)(2,1)} %q_ref.3), channel_id=1, source_target_pairs={{0,1},{1,0},{2,3},{3,2},{4,5},{5,4},{6,7},{7,6},{8,9},{9,8},{10,11... | collective-permute-start | bytes 1572872 | tf_op jit(solution)/shard_map/ppermute | solution.py:37
  11.6 10.4 %copy-start.1 = (bf16[512,512]{1,0:T(8,128)(2,1)S(1)}, bf16[512,512]{1,0:T(8,128)(2,1)}, u32[]{:S(2)}) copy-start(bf16[512,512]{1,0:T(8,128)(2,1)} %q_ref.3) | copy-start | bytes 1572868
  11.6 10.3 %copy-start.2 = (s32[4]{0:T(128)S(1)}, s32[4]{0:T(128)}, u32[]{:S(2)}) copy-start(s32[4]{0:T(128)} %doc_ref.3) | copy-start | bytes 52
  11.7 10.3 %copy-start.3 = (s32[1,35]{1,0:T(1,128)S(1)}, s32[1,35]{1,0:T(1,128)}, u32[]{:S(2)}) copy-start(s32[1,35]{1,0:T(1,128)} %list_ref.3) | copy-start | bytes 424
  11.9 6.2 %collective-permute-start.7 = (bf16[512,128]{1,0:T(8,128)(2,1)S(1)}, bf16[512,128]{1,0:T(8,128)(2,1)S(1)}, u32[]{:S(2)}, u32[]{:S(2)}) collective-permute-start(bf16[512,128]{1,0:T(8,128)(2,1)S(1)} %collective-permute-done.2.rest_1_), channel_id=1, source_target_pairs={{0,1},{1,0},{2,3},{3,2},{4,5},{5,4},{6,7},{7,6},{8,9},{9,8},{10,11... | collective-permute-start | bytes 393224 | tf_op jit(solution)/shard_map/ppermute | solution.py:37
  16.3 3.5 %collective-permute-start.6 = (bf16[512,128]{1,0:T(8,128)(2,1)S(1)}, bf16[512,128]{1,0:T(8,128)(2,1)S(1)}, u32[]{:S(2)}, u32[]{:S(2)}) collective-permute-start(bf16[512,128]{1,0:T(8,128)(2,1)S(1)} %collective-permute-done.1.rest_0_), channel_id=1, source_target_pairs={{0,1},{1,0},{2,3},{3,2},{4,5},{5,4},{6,7},{7,6},{8,9},{9,8},{10,11... | collective-permute-start | bytes 393224 | tf_op jit(solution)/shard_map/ppermute | solution.py:37
  16.5 12.0 %collective-permute-start.3 = (bf16[1024,128]{1,0:T(8,128)(2,1)S(1)}, bf16[1024,128]{1,0:T(8,128)(2,1)S(1)}, u32[]{:S(2)}, u32[]{:S(2)}) collective-permute-start(bf16[1024,128]{1,0:T(8,128)(2,1)S(1)} %pad_maximum_fusion), channel_id=1, source_target_pairs={{0,8},{1,9},{2,10},{3,11},{4,12},{5,13},{6,14},{7,15},{8,16},{9,17... | collective-permute-start | bytes 786440 | tf_op jit(solution)/shard_map/ppermute | solution.py:37
  18.1 13.3 %collective-permute-start.4 = (bf16[1024,128]{1,0:T(8,128)(2,1)S(1)}, bf16[1024,128]{1,0:T(8,128)(2,1)S(1)}, u32[]{:S(2)}, u32[]{:S(2)}) collective-permute-start(bf16[1024,128]{1,0:T(8,128)(2,1)S(1)} %pad_maximum_fusion.1), channel_id=1, source_target_pairs={{0,24},{1,25},{2,26},{3,27},{4,28},{5,29},{6,30},{7,31},{8,0},{9,1... | collective-permute-start | bytes 786440 | tf_op jit(solution)/shard_map/ppermute | solution.py:37
  19.8 13.3 %collective-permute-start.5 = (bf16[1024,128]{1,0:T(8,128)(2,1)S(1)}, bf16[1024,128]{1,0:T(8,128)(2,1)S(1)}, u32[]{:S(2)}, u32[]{:S(2)}) collective-permute-start(bf16[1024,128]{1,0:T(8,128)(2,1)S(1)} %pad_maximum_fusion.2), channel_id=1, source_target_pairs={{0,16},{1,17},{2,18},{3,19},{4,20},{5,21},{6,22},{7,23},{8,24},{9,... | collective-permute-start | bytes 786440 | tf_op jit(solution)/shard_map/ppermute | solution.py:37
  33.1 1.5 %collective-permute-start.8 = (bf16[1024,128]{1,0:T(8,128)(2,1)S(1)}, bf16[1024,128]{1,0:T(8,128)(2,1)S(1)}, u32[]{:S(2)}, u32[]{:S(2)}) collective-permute-start(bf16[1024,128]{1,0:T(8,128)(2,1)S(1)} %collective-permute-done.3.rest_0_), channel_id=1, source_target_pairs={{0,1},{1,0},{2,3},{3,2},{4,5},{5,4},{6,7},{7,6},{8,9},{9,8},{10,11... | collective-permute-start | bytes 786440 | tf_op jit(solution)/shard_map/ppermute | solution.py:37
  33.1 1.9 %collective-permute-start.9 = (bf16[1024,128]{1,0:T(8,128)(2,1)S(1)}, bf16[1024,128]{1,0:T(8,128)(2,1)S(1)}, u32[]{:S(2)}, u32[]{:S(2)}) collective-permute-start(bf16[1024,128]{1,0:T(8,128)(2,1)S(1)} %collective-permute-done.4.rest_1_), channel_id=1, source_target_pairs={{0,1},{1,0},{2,3},{3,2},{4,5},{5,4},{6,7},{7,6},{8,9},{9,8},{10,11... | collective-permute-start | bytes 786440 | tf_op jit(solution)/shard_map/ppermute | solution.py:37
  33.6 1.8 %collective-permute-start.10 = (bf16[1024,128]{1,0:T(8,128)(2,1)S(1)}, bf16[1024,128]{1,0:T(8,128)(2,1)S(1)}, u32[]{:S(2)}, u32[]{:S(2)}) collective-permute-start(bf16[1024,128]{1,0:T(8,128)(2,1)S(1)} %collective-permute-done.5.rest_2_), channel_id=1, source_target_pairs={{0,1},{1,0},{2,3},{3,2},{4,5},{5,4},{6,7},{7,6},{8,9},{9,8},{10,11... | collective-permute-start | bytes 786440 | tf_op jit(solution)/shard_map/ppermute | solution.py:37
  35.4 14.0 %copy-start = (bf16[512,2048]{1,0:T(8,128)(2,1)S(1)}, bf16[512,2048]{1,0:T(8,128)(2,1)}, u32[]{:S(2)}) copy-start(bf16[512,2048]{1,0:T(8,128)(2,1)} %w_ref.1) | copy-start | bytes 6291460
  47.4 2.0 %collective-permute-start.11 = (bf16[256,1024]{1,0:T(8,128)(2,1)S(1)}, bf16[256,1024]{1,0:T(8,128)(2,1)S(1)}, u32[]{:S(2)}, u32[]{:S(2)}) collective-permute-start(bf16[256,1024]{1,0:T(8,128)(2,1)S(1)} %far.1.ho_ref), channel_id=1, source_target_pairs={{0,1},{1,0},{2,3},{3,2},{4,5},{5,4},{6,7},{7,6},{8,9},{9,8},{10,11... | collective-permute-start | bytes 1572872 | tf_op jit(solution)/shard_map/ppermute | solution.py:37
  52.6 12.7 %collective-permute-start.13 = (bf16[512,256]{1,0:T(8,128)(2,1)S(1)}, bf16[512,256]{1,0:T(8,128)(2,1)S(1)}, u32[]{:S(2)}, u32[]{:S(2)}) collective-permute-start(bf16[512,256]{1,0:T(8,128)(2,1)S(1)} %get-tuple-element.31), channel_id=1, source_target_pairs={{0,2},{1,7},{2,4},{3,1},{4,6},{5,3},{6,0},{7,5},{8,10},{9,15},{10,... | collective-permute-start | bytes 786440 | tf_op jit(solution)/shard_map/ppermute | solution.py:37
  56.0 12.2 %collective-permute-start.15 = (bf16[512,256]{1,0:T(8,128)(2,1)S(1)}, bf16[512,256]{1,0:T(8,128)(2,1)S(1)}, u32[]{:S(2)}, u32[]{:S(2)}) collective-permute-start(bf16[512,256]{1,0:T(8,128)(2,1)S(1)} %get-tuple-element.32), channel_id=1, source_target_pairs={{0,2},{1,7},{2,4},{3,1},{4,6},{5,3},{6,0},{7,5},{8,10},{9,15},{10,... | collective-permute-start | bytes 786440 | tf_op jit(solution)/shard_map/ppermute | solution.py:37
  65.4 10.6 %collective-permute-start.14 = (bf16[512,256]{1,0:T(8,128)(2,1)S(1)}, bf16[512,256]{1,0:T(8,128)(2,1)S(1)}, u32[]{:S(2)}, u32[]{:S(2)}) collective-permute-start(bf16[512,256]{1,0:T(8,128)(2,1)S(1)} %add_convert_fusion.1), channel_id=1, source_target_pairs={{0,2},{1,7},{2,4},{3,1},{4,6},{5,3},{6,0},{7,5},{8,10},{9,15},{10,... | collective-permute-start | bytes 786440 | tf_op jit(solution)/shard_map/ppermute | solution.py:37
  68.1 7.8 %collective-permute-start.16 = (bf16[512,256]{1,0:T(8,128)(2,1)S(1)}, bf16[512,256]{1,0:T(8,128)(2,1)S(1)}, u32[]{:S(2)}, u32[]{:S(2)}) collective-permute-start(bf16[512,256]{1,0:T(8,128)(2,1)S(1)} %collective-permute-done.15), channel_id=1, source_target_pairs={{0,1},{1,0},{2,3},{3,2},{4,5},{5,4},{6,7},{7,6},{8,9},{9,8},{10,11... | collective-permute-start | bytes 786440 | tf_op jit(solution)/shard_map/ppermute | solution.py:37

commit v4 on v3

--- a/solution.py
+++ b/solution.py
@@ -219,13 +219,13 @@
 
     lax.fori_loop(0, 2, block, 0)
 
-def project_kernel(ho_ref, got_ref, w_ref, rw_ref, *rest):
-    outs = rest[:4]
-    ho, ws, sem = rest[4:]
+def project_kernel(first, last, ho_ref, got_ref, w_ref, rw_ref, *rest):
+    outs = rest[: last - first]
+    ho, ws, sem = rest[last - first :]
     ctx, z, core = position()
     copies = Copies(sem)
     dz = jnp.where(core == 0, 1, 3)
-    wanted = ((2, core), (dz, 1 - core), (dz, core), (0, core))
+    wanted = ((2, core), (dz, 1 - core), (dz, core), (0, core))[first:last]
     mine = pl.ds(pl.multiple_of(core * HALF, HALF), HALF)
     theirs = pl.ds(pl.multiple_of((1 - core) * HALF, HALF), HALF)
     copies.start(ho_ref, ho.at[mine])
@@ -300,23 +300,24 @@
     return call(far_kernel, "far", [out], scratch, 6 * SHARD, HALF, args)[0]
 
 
-def project(*args):
+def project(first, last, *args):
+    count = last - first
     out = jax.ShapeDtypeStruct((SHARD, PIECE), jnp.bfloat16)
     return pl.pallas_call(
-        project_kernel,
-        out_shape=[out] * 4,
+        functools.partial(project_kernel, first, last),
+        out_shape=[out] * count,
         in_specs=[ANY] * 4,
-        out_specs=[VMEM] * 4,
+        out_specs=[VMEM] * count,
         scratch_shapes=[
             pltpu.VMEM((SHARD, 1024), jnp.bfloat16),
-            pltpu.VMEM((4, 1024, PIECE), jnp.bfloat16),
-            pltpu.SemaphoreType.DMA((11,)),
+            pltpu.VMEM((count, 1024, PIECE), jnp.bfloat16),
+            pltpu.SemaphoreType.DMA((3 + 2 * count,)),
         ],
         compiler_params=pltpu.CompilerParams(vmem_limit_bytes=GRANT),
         cost_estimate=pl.CostEstimate(
-            flops=10**9, bytes_accessed=4 * 2**20, transcendentals=0
+            flops=count * 2**28, bytes_accessed=count * 2**20, transcendentals=0
         ),
-        name="project",
+        name=f"project{first}",
     )(*args)
 
 
@@ -361,8 +362,11 @@
     *turns, acc = lax.optimization_barrier((*turns, acc))
     turns += [go(t, other_core) for t in turns]
     ho = far(doc_start, block_list, queries, rq, *turns, acc, ml)
-    relay, plain, fwd, keep = project(ho, go(ho, other_core), out_weight, rw)
+    got = go(ho, other_core)
+    relay, plain = project(0, 2, ho, got, out_weight, rw)
+    relay, plain, got = lax.optimization_barrier((relay, plain, got))
     came = go(relay, along_z(n_head))
+    fwd, keep = project(2, 4, ho, got, out_weight, rw)
     beyond = go(plain, along_z(n_head))
     summed = go(f32_sum(fwd, came), along_z(n_head))
     return f32_sum(keep, summed, go(beyond, other_core))

time: 77 us -> 75.4 us (0.979)
  waiting for transfers between devices: 27.1 us -> 25.4 us
    ppermute x17, waiting for transfers between devices: 27.1 us -> 25.4 us  [send(): return lax.ppermute(block, AXES, ctx_head_pairs(n_ctx, n_head, route))]
    pallas_call x1 -> x2, Pallas kernels: 3.26 us -> 3.36 us  [project(): pl.pallas_call(functools.partial(project_kernel, first, last), out_shape=...]
  transfers between devices with their start and end apart: 17 -> 17, of which waited for: 11 -> 11; matrix products, arithmetic and copies ran while one was open for 2% -> 3% of each run, Pallas kernels for 24% -> 27%
where the time goes in v4:
time: 75.4 us; the launch traced here: 75.2 us
  waiting for transfers between devices  25.4 us (34%)
  starting transfers between devices  23.1 us (31%)
  Pallas kernels  21.8 us (29%)
  local copies, waits for them, and re-layouts  2.98 us (4%)
  other arithmetic  1.73 us (2%)
    ppermute x17, waiting for transfers between devices, send(): return lax.ppermute(block, AXES, ctx_head_pairs(n_ctx, n_head, route))  25.4 us
    ppermute x17, starting transfers between devices, send(): return lax.ppermute(block, AXES, ctx_head_pairs(n_ctx, n_head, route))  23.1 us
    pallas_call x2, Pallas kernels, call(): pl.pallas_call(kernel, out_shape=out_shape, in_specs=[SMEM, SMEM] + [ANY]...  18.4 us
    pallas_call x2, Pallas kernels, project(): pl.pallas_call(functools.partial(project_kernel, first, last), out_shape=...  3.36 us
    dynamic_slice x2, local copies, waits for them, and re-layouts, on_device(): lax.dynamic_index_in_dim(a, z, 1, keepdims=False)  1.59 us
  transfers between devices with their start and end apart: 17, of which 11 were waited for; matrix products, arithmetic and copies ran while one was open for 3% of the time, Pallas kernels for 27%

profile of v4, /device:TPU:32, one launch (start us, length us, event | category | flops | bytes accessed | tf_op | source)
XLA Modules:
  0.0 75.2 jit_solution(10524284746937111144)
XLA Ops:
  0.0 1.3 %constant_dynamic-slice_fusion.2 = (bf16[256,1,128]{2,1,0:T(2,128)(2,1)S(1)}, bf16[256,1,128]{2,1,0:T(2,128)(2,1)S(1)}) fusion(bf16[512,4,128]{2,1,0:T(4,128)(2,1)} %param.8, s32[]{:T(128)S(6)} %select_n.64, s32[]{:T(128)S(6)} %select_n.67, bf16[512,4,128]{2,1,0:T(4,128)(2,1)} %param.7), kind=kLoop, calls=%fused_computation.18 | loop fusion | bytes 262152 | tf_op jit(solution)/shard_map/dynamic_slice | solution.py:342
  1.3 0.0 copy-start.4
  1.4 0.7 pad_maximum_fusion.3
  2.0 5.1 %collective-permute-start.2 = (bf16[512,128]{1,0:T(8,128)(2,1)}, bf16[512,128]{1,0:T(8,128)(2,1)S(1)}, u32[]{:S(2)}, u32[]{:S(2)}) collective-permute-start(bf16[512,128]{1,0:T(8,128)(2,1)} %pad_maximum_fusion.3), channel_id=1, source_target_pairs={{0,64},{1,65},{2,66},{3,67},{4,68},{5,69},{6,70},{7,71},{8,72},{9,... | collective-permute-start | bytes 393224 | tf_op jit(solution)/shard_map/ppermute | solution.py:37
  7.1 2.6 %collective-permute-start.1 = (bf16[512,128]{1,0:T(8,128)(2,1)}, bf16[512,128]{1,0:T(8,128)(2,1)S(1)}, u32[]{:S(2)}, u32[]{:S(2)}) collective-permute-start(bf16[512,128]{1,0:T(8,128)(2,1)} %pad_maximum_fusion.3), channel_id=1, source_target_pairs={{0,32},{1,33},{2,34},{3,35},{4,36},{5,37},{6,38},{7,39},{8,40},{9,... | collective-permute-start | bytes 393224 | tf_op jit(solution)/shard_map/ppermute | solution.py:37
  9.7 0.1 collective-permute-start.12
  9.8 0.5 collective-permute-start
  10.3 1.3 %constant_dynamic-slice_fusion.1 = bf16[512,1,128]{2,1,0:T(2,128)(2,1)S(1)} fusion(bf16[512,4,128]{2,1,0:T(4,128)(2,1)} %param.7, s32[]{:T(128)S(6)} %select_n.66), kind=kLoop, calls=%fused_computation.17 | loop fusion | bytes 262148 | tf_op jit(solution)/shard_map/jit(dynamic_index_in_dim)/dynamic_slice | solution.py:338
  11.6 0.0 copy-start.1
  11.6 0.0 copy-start.2
  11.7 0.0 copy-start.3
  11.7 0.2 collective-permute-done.2.rest_1_
  11.9 0.0 collective-permute-start.7
  11.9 4.4 %collective-permute-done.1.rest_0_ = bf16[512,128]{1,0:T(8,128)(2,1)S(1)} collective-permute-done((bf16[512,128]{1,0:T(8,128)(2,1)}, bf16[512,128]{1,0:T(8,128)(2,1)S(1)}, u32[]{:S(2)}, u32[]{:S(2)}) %collective-permute-start.1) | collective-permute-done | bytes 131104 | tf_op jit(solution)/shard_map/ppermute | solution.py:37
  16.3 0.0 collective-permute-start.6
  16.3 0.1 broadcast_select_fusion.1
  16.5 1.6 %collective-permute-start.3 = (bf16[1024,128]{1,0:T(8,128)(2,1)S(1)}, bf16[1024,128]{1,0:T(8,128)(2,1)S(1)}, u32[]{:S(2)}, u32[]{:S(2)}) collective-permute-start(bf16[1024,128]{1,0:T(8,128)(2,1)S(1)} %pad_maximum_fusion), channel_id=1, source_target_pairs={{0,8},{1,9},{2,10},{3,11},{4,12},{5,13},{6,14},{7,15},{8,16},{9,17... | collective-permute-start | bytes 786440 | tf_op jit(solution)/shard_map/ppermute | solution.py:37
  18.1 0.0 collective-permute-done.7.rest_3_
  18.1 1.7 %collective-permute-start.4 = (bf16[1024,128]{1,0:T(8,128)(2,1)S(1)}, bf16[1024,128]{1,0:T(8,128)(2,1)S(1)}, u32[]{:S(2)}, u32[]{:S(2)}) collective-permute-start(bf16[1024,128]{1,0:T(8,128)(2,1)S(1)} %pad_maximum_fusion.1), channel_id=1, source_target_pairs={{0,24},{1,25},{2,26},{3,27},{4,28},{5,29},{6,30},{7,31},{8,0},{9,1... | collective-permute-start | bytes 786440 | tf_op jit(solution)/shard_map/ppermute | solution.py:37
  19.8 0.0 collective-permute-done.6.rest_2_
  19.8 1.8 %collective-permute-start.5 = (bf16[1024,128]{1,0:T(8,128)(2,1)S(1)}, bf16[1024,128]{1,0:T(8,128)(2,1)S(1)}, u32[]{:S(2)}, u32[]{:S(2)}) collective-permute-start(bf16[1024,128]{1,0:T(8,128)(2,1)S(1)} %pad_maximum_fusion.2), channel_id=1, source_target_pairs={{0,16},{1,17},{2,18},{3,19},{4,20},{5,21},{6,22},{7,23},{8,24},{9,... | collective-permute-start | bytes 786440 | tf_op jit(solution)/shard_map/ppermute | solution.py:37
  21.7 0.3 constant_dynamic-slice_fusion
  22.0 6.5 %near.1 = (f32[256,1024]{1,0:T(8,128)S(1)}, f32[256,128]{1,0:T(8,128)S(1)}) custom-call(s32[4]{0:T(128)S(1)} %copy-done.2, s32[1,35]{1,0:T(1,128)S(1)} %copy-done.3, bf16[512,512]{1,0:T(8,128)(2,1)S(1)} %copy-done.1, bf16[512,512]{1,0:T(8,128)(2,1)S(1)} %collective-permute-done.rq_ref, bf16[512,128]{1,0:T(8,128)(2,1)S(1)} %bitcast.12, ...), custom_call_target="tpu_custom_call" | custom-call | flops 1610612736 | bytes 4194304 | tf_op jit(solution)/shard_map/near/pallas_call | solution.py:266
  28.5 0.0 collective-permute-done.3.rest_0_
  28.5 2.9 %collective-permute-done.4.rest_1_ = bf16[1024,128]{1,0:T(8,128)(2,1)S(1)} collective-permute-done((bf16[1024,128]{1,0:T(8,128)(2,1)S(1)}, bf16[1024,128]{1,0:T(8,128)(2,1)S(1)}, u32[]{:S(2)}, u32[]{:S(2)}) %collective-permute-start.4) | collective-permute-done | bytes 262176 | tf_op jit(solution)/shard_map/ppermute | solution.py:37
  31.4 1.7 %collective-permute-done.5.rest_2_ = bf16[1024,128]{1,0:T(8,128)(2,1)S(1)} collective-permute-done((bf16[1024,128]{1,0:T(8,128)(2,1)S(1)}, bf16[1024,128]{1,0:T(8,128)(2,1)S(1)}, u32[]{:S(2)}, u32[]{:S(2)}) %collective-permute-start.5) | collective-permute-done | bytes 262176 | tf_op jit(solution)/shard_map/ppermute | solution.py:37
  33.1 0.0 collective-permute-start.8
  33.1 0.5 collective-permute-start.9
  33.6 0.0 collective-permute-start.10
  33.6 1.0 %collective-permute-done.8.rest_3_ = bf16[1024,128]{1,0:T(8,128)(2,1)S(1)} collective-permute-done((bf16[1024,128]{1,0:T(8,128)(2,1)S(1)}, bf16[1024,128]{1,0:T(8,128)(2,1)S(1)}, u32[]{:S(2)}, u32[]{:S(2)}) %collective-permute-start.8) | collective-permute-done | bytes 262176 | tf_op jit(solution)/shard_map/ppermute | solution.py:37
  34.7 0.4 collective-permute-done.9.rest_4_
  35.0 0.4 collective-permute-done.10.rest_5_
  35.4 11.9 %far.1.ho_ref = bf16[256,1024]{1,0:T(8,128)(2,1)S(1)} custom-call(s32[4]{0:T(128)S(1)} %copy-done.2, s32[1,35]{1,0:T(1,128)S(1)} %copy-done.3, bf16[512,512]{1,0:T(8,128)(2,1)S(1)} %copy-done.1, bf16[512,512]{1,0:T(8,128)(2,1)S(1)} %collective-permute-done.rq_ref, bf16[1024,128]{1,0:T(8,128)(2,1)S(1)} %collective-permute-done.3.rest_0_, ...), custom_call_target="tpu_custom_call" | custom-call | flops 3221225472 | bytes 4194304 | tf_op jit(solution)/shard_map/far/pallas_call | solution.py:266
  47.4 0.2 collective-permute-start.11
  47.6 1.8 %collective-permute-done.11.got_ref = bf16[256,1024]{1,0:T(8,128)(2,1)S(1)} collective-permute-done((bf16[256,1024]{1,0:T(8,128)(2,1)S(1)}, bf16[256,1024]{1,0:T(8,128)(2,1)S(1)}, u32[]{:S(2)}, u32[]{:S(2)}) %collective-permute-start.11) | collective-permute-done | bytes 524320 | tf_op jit(solution)/shard_map/ppermute | solution.py:37
  49.4 0.0 collective-permute-done.12.rw_ref
  49.4 1.7 %project0.1 = (bf16[512,256]{1,0:T(8,128)(2,1)S(1)}, bf16[512,256]{1,0:T(8,128)(2,1)S(1)}) custom-call(bf16[256,1024]{1,0:T(8,128)(2,1)S(1)} %far.1.ho_ref, bf16[256,1024]{1,0:T(8,128)(2,1)S(1)} %collective-permute-done.11.got_ref, bf16[512,2048]{1,0:T(8,128)(2,1)S(1)} %copy-done, bf16[512,2048]{1,0:T(8,128)(2,1)S(1)} %collective-permute-done.12.rw_ref), custom_call_target="tpu_custom_call" | custom-call | flops 536870912 | bytes 2097152 | tf_op jit(solution)/shard_map/project0/pallas_call | solution.py:306
  51.1 3.3 %collective-permute-start.13 = (bf16[512,256]{1,0:T(8,128)(2,1)S(1)}, bf16[512,256]{1,0:T(8,128)(2,1)S(1)}, u32[]{:S(2)}, u32[]{:S(2)}) collective-permute-start(bf16[512,256]{1,0:T(8,128)(2,1)S(1)} %get-tuple-element.37), channel_id=1, source_target_pairs={{0,2},{1,7},{2,4},{3,1},{4,6},{5,3},{6,0},{7,5},{8,10},{9,15},{10,... | collective-permute-start | bytes 786440 | tf_op jit(solution)/shard_map/ppermute | solution.py:37
  54.4 3.6 %collective-permute-start.15 = (bf16[512,256]{1,0:T(8,128)(2,1)S(1)}, bf16[512,256]{1,0:T(8,128)(2,1)S(1)}, u32[]{:S(2)}, u32[]{:S(2)}) collective-permute-start(bf16[512,256]{1,0:T(8,128)(2,1)S(1)} %get-tuple-element.38), channel_id=1, source_target_pairs={{0,2},{1,7},{2,4},{3,1},{4,6},{5,3},{6,0},{7,5},{8,10},{9,15},{10,... | collective-permute-start | bytes 786440 | tf_op jit(solution)/shard_map/ppermute | solution.py:37
  58.0 1.7 %project2.1 = (bf16[512,256]{1,0:T(8,128)(2,1)S(1)}, bf16[512,256]{1,0:T(8,128)(2,1)S(1)}) custom-call(bf16[256,1024]{1,0:T(8,128)(2,1)S(1)} %far.1.ho_ref, bf16[256,1024]{1,0:T(8,128)(2,1)S(1)} %collective-permute-done.11.got_ref, bf16[512,2048]{1,0:T(8,128)(2,1)S(1)} %copy-done, bf16[512,2048]{1,0:T(8,128)(2,1)S(1)} %collective-permute-done.12.rw_ref), custom_call_target="tpu_custom_call" | custom-call | flops 536870912 | bytes 2097152 | tf_op jit(solution)/shard_map/project2/pallas_call | solution.py:306
  59.7 4.0 %collective-permute-done.13 = bf16[512,256]{1,0:T(8,128)(2,1)S(1)} collective-permute-done((bf16[512,256]{1,0:T(8,128)(2,1)S(1)}, bf16[512,256]{1,0:T(8,128)(2,1)S(1)}, u32[]{:S(2)}, u32[]{:S(2)}) %collective-permute-start.13) | collective-permute-done | bytes 262176 | tf_op jit(solution)/shard_map/ppermute | solution.py:37
  63.7 0.1 add_convert_fusion.1
  63.8 0.9 %collective-permute-start.14 = (bf16[512,256]{1,0:T(8,128)(2,1)S(1)}, bf16[512,256]{1,0:T(8,128)(2,1)S(1)}, u32[]{:S(2)}, u32[]{:S(2)}) collective-permute-start(bf16[512,256]{1,0:T(8,128)(2,1)S(1)} %add_convert_fusion.1), channel_id=1, source_target_pairs={{0,2},{1,7},{2,4},{3,1},{4,6},{5,3},{6,0},{7,5},{8,10},{9,15},{10,... | collective-permute-start | bytes 786440 | tf_op jit(solution)/shard_map/ppermute | solution.py:37
  64.7 1.8 %collective-permute-done.15 = bf16[512,256]{1,0:T(8,128)(2,1)S(1)} collective-permute-done((bf16[512,256]{1,0:T(8,128)(2,1)S(1)}, bf16[512,256]{1,0:T(8,128)(2,1)S(1)}, u32[]{:S(2)}, u32[]{:S(2)}) %collective-permute-start.15) | collective-permute-done | bytes 262176 | tf_op jit(solution)/shard_map/ppermute | solution.py:37
  66.6 1.1 %collective-permute-start.16 = (bf16[512,256]{1,0:T(8,128)(2,1)S(1)}, bf16[512,256]{1,0:T(8,128)(2,1)S(1)}, u32[]{:S(2)}, u32[]{:S(2)}) collective-permute-start(bf16[512,256]{1,0:T(8,128)(2,1)S(1)} %collective-permute-done.15), channel_id=1, source_target_pairs={{0,1},{1,0},{2,3},{3,2},{4,5},{5,4},{6,7},{7,6},{8,9},{9,8},{10,11... | collective-permute-start | bytes 786440 | tf_op jit(solution)/shard_map/ppermute | solution.py:37
  67.6 6.8 %collective-permute-done.14 = bf16[512,256]{1,0:T(8,128)(2,1)S(1)} collective-permute-done((bf16[512,256]{1,0:T(8,128)(2,1)S(1)}, bf16[512,256]{1,0:T(8,128)(2,1)S(1)}, u32[]{:S(2)}, u32[]{:S(2)}) %collective-permute-start.14) | collective-permute-done | bytes 262176 | tf_op jit(solution)/shard_map/ppermute | solution.py:37
  74.4 0.0 collective-permute-done.16
  74.4 0.8 %add_convert_fusion = bf16[512,256]{1,0:T(8,128)(2,1)} fusion(bf16[512,256]{1,0:T(8,128)(2,1)S(1)} %collective-permute-done.16, bf16[512,256]{1,0:T(8,128)(2,1)S(1)} %collective-permute-done.14, bf16[512,256]{1,0:T(8,128)(2,1)S(1)} %get-tuple-element.35), kind=kLoop, calls=%fused_computation | loop fusion | flops 786432 | bytes 1048576 | tf_op jit(solution)/shard_map/convert_element_type | solution.py:325
  (14 shorter events, 0.1 us)
Async XLA Ops:
  1.3 20.3 %copy-start.4 = (bf16[512,4,128]{2,1,0:T(4,128)(2,1)S(1)}, bf16[512,4,128]{2,1,0:T(4,128)(2,1)}, u32[]{:S(2)}) copy-start(bf16[512,4,128]{2,1,0:T(4,128)(2,1)} %param.8) | copy-start | bytes 1572868
  2.0 9.8 %collective-permute-start.2 = (bf16[512,128]{1,0:T(8,128)(2,1)}, bf16[512,128]{1,0:T(8,128)(2,1)S(1)}, u32[]{:S(2)}, u32[]{:S(2)}) collective-permute-start(bf16[512,128]{1,0:T(8,128)(2,1)} %pad_maximum_fusion.3), channel_id=1, source_target_pairs={{0,64},{1,65},{2,66},{3,67},{4,68},{5,69},{6,70},{7,71},{8,72},{9,... | collective-permute-start | bytes 393224 | tf_op jit(solution)/shard_map/ppermute | solution.py:37
  7.1 9.2 %collective-permute-start.1 = (bf16[512,128]{1,0:T(8,128)(2,1)}, bf16[512,128]{1,0:T(8,128)(2,1)S(1)}, u32[]{:S(2)}, u32[]{:S(2)}) collective-permute-start(bf16[512,128]{1,0:T(8,128)(2,1)} %pad_maximum_fusion.3), channel_id=1, source_target_pairs={{0,32},{1,33},{2,34},{3,35},{4,36},{5,37},{6,38},{7,39},{8,40},{9,... | collective-permute-start | bytes 393224 | tf_op jit(solution)/shard_map/ppermute | solution.py:37
  9.7 39.7 %collective-permute-start.12 = (bf16[512,2048]{1,0:T(8,128)(2,1)}, bf16[512,2048]{1,0:T(8,128)(2,1)S(1)}, u32[]{:S(2)}, u32[]{:S(2)}) collective-permute-start(bf16[512,2048]{1,0:T(8,128)(2,1)} %w_ref.3), channel_id=1, source_target_pairs={{0,1},{1,0},{2,3},{3,2},{4,5},{5,4},{6,7},{7,6},{8,9},{9,8},{10,11... | collective-permute-start | bytes 6291464 | tf_op jit(solution)/shard_map/ppermute | solution.py:37
  9.8 12.2 %collective-permute-start = (bf16[512,512]{1,0:T(8,128)(2,1)}, bf16[512,512]{1,0:T(8,128)(2,1)S(1)}, u32[]{:S(2)}, u32[]{:S(2)}) collective-permute-start(bf16[512,512]{1,0:T(8,128)(2,1)} %q_ref.3), channel_id=1, source_target_pairs={{0,1},{1,0},{2,3},{3,2},{4,5},{5,4},{6,7},{7,6},{8,9},{9,8},{10,11... | collective-permute-start | bytes 1572872 | tf_op jit(solution)/shard_map/ppermute | solution.py:37
  11.6 10.4 %copy-start.1 = (bf16[512,512]{1,0:T(8,128)(2,1)S(1)}, bf16[512,512]{1,0:T(8,128)(2,1)}, u32[]{:S(2)}) copy-start(bf16[512,512]{1,0:T(8,128)(2,1)} %q_ref.3) | copy-start | bytes 1572868
  11.6 10.3 %copy-start.2 = (s32[4]{0:T(128)S(1)}, s32[4]{0:T(128)}, u32[]{:S(2)}) copy-start(s32[4]{0:T(128)} %doc_ref.3) | copy-start | bytes 52
  11.7 10.3 %copy-start.3 = (s32[1,35]{1,0:T(1,128)S(1)}, s32[1,35]{1,0:T(1,128)}, u32[]{:S(2)}) copy-start(s32[1,35]{1,0:T(1,128)} %list_ref.3) | copy-start | bytes 424
  11.9 6.2 %collective-permute-start.7 = (bf16[512,128]{1,0:T(8,128)(2,1)S(1)}, bf16[512,128]{1,0:T(8,128)(2,1)S(1)}, u32[]{:S(2)}, u32[]{:S(2)}) collective-permute-start(bf16[512,128]{1,0:T(8,128)(2,1)S(1)} %collective-permute-done.2.rest_1_), channel_id=1, source_target_pairs={{0,1},{1,0},{2,3},{3,2},{4,5},{5,4},{6,7},{7,6},{8,9},{9,8},{10,11... | collective-permute-start | bytes 393224 | tf_op jit(solution)/shard_map/ppermute | solution.py:37
  16.3 3.5 %collective-permute-start.6 = (bf16[512,128]{1,0:T(8,128)(2,1)S(1)}, bf16[512,128]{1,0:T(8,128)(2,1)S(1)}, u32[]{:S(2)}, u32[]{:S(2)}) collective-permute-start(bf16[512,128]{1,0:T(8,128)(2,1)S(1)} %collective-permute-done.1.rest_0_), channel_id=1, source_target_pairs={{0,1},{1,0},{2,3},{3,2},{4,5},{5,4},{6,7},{7,6},{8,9},{9,8},{10,11... | collective-permute-start | bytes 393224 | tf_op jit(solution)/shard_map/ppermute | solution.py:37
  16.5 12.0 %collective-permute-start.3 = (bf16[1024,128]{1,0:T(8,128)(2,1)S(1)}, bf16[1024,128]{1,0:T(8,128)(2,1)S(1)}, u32[]{:S(2)}, u32[]{:S(2)}) collective-permute-start(bf16[1024,128]{1,0:T(8,128)(2,1)S(1)} %pad_maximum_fusion), channel_id=1, source_target_pairs={{0,8},{1,9},{2,10},{3,11},{4,12},{5,13},{6,14},{7,15},{8,16},{9,17... | collective-permute-start | bytes 786440 | tf_op jit(solution)/shard_map/ppermute | solution.py:37
  18.1 13.3 %collective-permute-start.4 = (bf16[1024,128]{1,0:T(8,128)(2,1)S(1)}, bf16[1024,128]{1,0:T(8,128)(2,1)S(1)}, u32[]{:S(2)}, u32[]{:S(2)}) collective-permute-start(bf16[1024,128]{1,0:T(8,128)(2,1)S(1)} %pad_maximum_fusion.1), channel_id=1, source_target_pairs={{0,24},{1,25},{2,26},{3,27},{4,28},{5,29},{6,30},{7,31},{8,0},{9,1... | collective-permute-start | bytes 786440 | tf_op jit(solution)/shard_map/ppermute | solution.py:37
  19.8 13.3 %collective-permute-start.5 = (bf16[1024,128]{1,0:T(8,128)(2,1)S(1)}, bf16[1024,128]{1,0:T(8,128)(2,1)S(1)}, u32[]{:S(2)}, u32[]{:S(2)}) collective-permute-start(bf16[1024,128]{1,0:T(8,128)(2,1)S(1)} %pad_maximum_fusion.2), channel_id=1, source_target_pairs={{0,16},{1,17},{2,18},{3,19},{4,20},{5,21},{6,22},{7,23},{8,24},{9,... | collective-permute-start | bytes 786440 | tf_op jit(solution)/shard_map/ppermute | solution.py:37
  33.1 1.5 %collective-permute-start.8 = (bf16[1024,128]{1,0:T(8,128)(2,1)S(1)}, bf16[1024,128]{1,0:T(8,128)(2,1)S(1)}, u32[]{:S(2)}, u32[]{:S(2)}) collective-permute-start(bf16[1024,128]{1,0:T(8,128)(2,1)S(1)} %collective-permute-done.3.rest_0_), channel_id=1, source_target_pairs={{0,1},{1,0},{2,3},{3,2},{4,5},{5,4},{6,7},{7,6},{8,9},{9,8},{10,11... | collective-permute-start | bytes 786440 | tf_op jit(solution)/shard_map/ppermute | solution.py:37
  33.1 1.9 %collective-permute-start.9 = (bf16[1024,128]{1,0:T(8,128)(2,1)S(1)}, bf16[1024,128]{1,0:T(8,128)(2,1)S(1)}, u32[]{:S(2)}, u32[]{:S(2)}) collective-permute-start(bf16[1024,128]{1,0:T(8,128)(2,1)S(1)} %collective-permute-done.4.rest_1_), channel_id=1, source_target_pairs={{0,1},{1,0},{2,3},{3,2},{4,5},{5,4},{6,7},{7,6},{8,9},{9,8},{10,11... | collective-permute-start | bytes 786440 | tf_op jit(solution)/shard_map/ppermute | solution.py:37
  33.6 1.8 %collective-permute-start.10 = (bf16[1024,128]{1,0:T(8,128)(2,1)S(1)}, bf16[1024,128]{1,0:T(8,128)(2,1)S(1)}, u32[]{:S(2)}, u32[]{:S(2)}) collective-permute-start(bf16[1024,128]{1,0:T(8,128)(2,1)S(1)} %collective-permute-done.5.rest_2_), channel_id=1, source_target_pairs={{0,1},{1,0},{2,3},{3,2},{4,5},{5,4},{6,7},{7,6},{8,9},{9,8},{10,11... | collective-permute-start | bytes 786440 | tf_op jit(solution)/shard_map/ppermute | solution.py:37
  35.4 14.0 %copy-start = (bf16[512,2048]{1,0:T(8,128)(2,1)S(1)}, bf16[512,2048]{1,0:T(8,128)(2,1)}, u32[]{:S(2)}) copy-start(bf16[512,2048]{1,0:T(8,128)(2,1)} %w_ref.3) | copy-start | bytes 6291460
  47.4 2.0 %collective-permute-start.11 = (bf16[256,1024]{1,0:T(8,128)(2,1)S(1)}, bf16[256,1024]{1,0:T(8,128)(2,1)S(1)}, u32[]{:S(2)}, u32[]{:S(2)}) collective-permute-start(bf16[256,1024]{1,0:T(8,128)(2,1)S(1)} %far.1.ho_ref), channel_id=1, source_target_pairs={{0,1},{1,0},{2,3},{3,2},{4,5},{5,4},{6,7},{7,6},{8,9},{9,8},{10,11... | collective-permute-start | bytes 1572872 | tf_op jit(solution)/shard_map/ppermute | solution.py:37
  51.1 12.7 %collective-permute-start.13 = (bf16[512,256]{1,0:T(8,128)(2,1)S(1)}, bf16[512,256]{1,0:T(8,128)(2,1)S(1)}, u32[]{:S(2)}, u32[]{:S(2)}) collective-permute-start(bf16[512,256]{1,0:T(8,128)(2,1)S(1)} %get-tuple-element.37), channel_id=1, source_target_pairs={{0,2},{1,7},{2,4},{3,1},{4,6},{5,3},{6,0},{7,5},{8,10},{9,15},{10,... | collective-permute-start | bytes 786440 | tf_op jit(solution)/shard_map/ppermute | solution.py:37
  54.4 12.1 %collective-permute-start.15 = (bf16[512,256]{1,0:T(8,128)(2,1)S(1)}, bf16[512,256]{1,0:T(8,128)(2,1)S(1)}, u32[]{:S(2)}, u32[]{:S(2)}) collective-permute-start(bf16[512,256]{1,0:T(8,128)(2,1)S(1)} %get-tuple-element.38), channel_id=1, source_target_pairs={{0,2},{1,7},{2,4},{3,1},{4,6},{5,3},{6,0},{7,5},{8,10},{9,15},{10,... | collective-permute-start | bytes 786440 | tf_op jit(solution)/shard_map/ppermute | solution.py:37
  63.8 10.6 %collective-permute-start.14 = (bf16[512,256]{1,0:T(8,128)(2,1)S(1)}, bf16[512,256]{1,0:T(8,128)(2,1)S(1)}, u32[]{:S(2)}, u32[]{:S(2)}) collective-permute-start(bf16[512,256]{1,0:T(8,128)(2,1)S(1)} %add_convert_fusion.1), channel_id=1, source_target_pairs={{0,2},{1,7},{2,4},{3,1},{4,6},{5,3},{6,0},{7,5},{8,10},{9,15},{10,... | collective-permute-start | bytes 786440 | tf_op jit(solution)/shard_map/ppermute | solution.py:37
  66.6 7.8 %collective-permute-start.16 = (bf16[512,256]{1,0:T(8,128)(2,1)S(1)}, bf16[512,256]{1,0:T(8,128)(2,1)S(1)}, u32[]{:S(2)}, u32[]{:S(2)}) collective-permute-start(bf16[512,256]{1,0:T(8,128)(2,1)S(1)} %collective-permute-done.15), channel_id=1, source_target_pairs={{0,1},{1,0},{2,3},{3,2},{4,5},{5,4},{6,7},{7,6},{8,9},{9,8},{10,11... | collective-permute-start | bytes 786440 | tf_op jit(solution)/shard_map/ppermute | solution.py:37
